TPU v7x, 32 devices: a whole 2x2x4 slice. The times are simulated.
32 devices in a mesh: seq: 16 (over z, x, core), head: 2 (over y).
Axes of the slice: x: 2, y: 2, z: 4, core: 2. Of those that a mesh axis runs over, the one named last changes fastest.
Arguments:
- queries: bfloat16 [4096, 5120], P('seq', 'head'), may hold values from -6 to 6
- keys_in: bfloat16 [4096, 5120], P('seq', 'head'), may hold values from -6 to 6
- values_in: bfloat16 [4096, 5120], P('seq', 'head'), may hold values from -162 to 162
- gain: bfloat16 [5120], P('head'), may hold values from 0.5 to 1.5
- upstream: bfloat16 [4096, 5120], P('seq', 'head'), may hold values from -6 to 6
Outputs:
- normed: bfloat16 [4096, 5120], P('seq', 'head')
- grad_queries: bfloat16 [4096, 5120], P('seq', 'head')
- grad_keys: bfloat16 [4096, 5120], P('seq', 'head')
- grad_values: bfloat16 [4096, 5120], P('seq', 'head')
All inputs are finite; a program needn't handle non-finite values.
Results may differ from a plain program's by a relative error of at most 0.015.
Values may be sent and summed in bfloat16 or wider, within the bound.
A program may use at most 192 MiB of HBM per device.

v0:
```python
import jax
import jax.numpy as jnp
from jax import lax
from jax.sharding import PartitionSpec as P

HEAD_WIDTH = 128
BLK = 64
LEV = 5


LOG_TWO = 0.6931471805599453
EPSILON = 1e-06


def padded_2(block, sides, width):
    for axis, dim in sides:
        count = lax.axis_size(axis)
        forward = [(i, i + 1) for i in range(count - 1)]
        backward = [(target, source) for source, target in forward]
        low = lax.ppermute(
            lax.slice_in_dim(block, block.shape[dim] - width, None, axis=dim), axis, forward
        )
        high = lax.ppermute(lax.slice_in_dim(block, 0, width, axis=dim), axis, backward)
        block = jnp.concatenate([low, block, high], axis=dim)
    return block


def partner_2(x, axis, bit):
    return lax.ppermute(x, axis, [(i, i ^ 1 << bit) for i in range(lax.axis_size(axis))])


def coarsen(tile):
    row_count = tile.shape[-2]
    pairs = tile.astype(jnp.float32).reshape(tile.shape[:-2] + (row_count // 2, 2, tile.shape[-1]))
    return (0.5 * (pairs[..., 0, :] + pairs[..., 1, :])).astype(jnp.bfloat16)


def spread(grad_tile):
    return 0.5 * jnp.repeat(grad_tile, 2, axis=grad_tile.ndim - 2)


def body(queries, keys_in, values_in, gain, upstream):
    row_count, col_count = queries.shape
    head_count = col_count // HEAD_WIDTH
    nblock = row_count // BLK
    seq_index = lax.axis_index("seq")
    seq_count = lax.axis_size("seq")
    score_scale = HEAD_WIDTH ** (-0.5)
    edge_cols = 3 * BLK
    middle_cols = 4 * BLK
    stacked = jnp.stack([keys_in, values_in], 0)
    padded = padded_2(stacked, (("seq", 1),), BLK)
    band_kv = jnp.stack(
        [
            padded[:, offset * BLK : offset * BLK + row_count].reshape(2, nblock, BLK, col_count)
            for offset in range(3)
        ],
        2,
    )
    band_kv = band_kv.reshape(2, nblock, 3 * BLK, head_count, HEAD_WIDTH)
    level_one = coarsen(stacked)
    lower_tile = level_one[:, :BLK]
    upper_tile = level_one[:, BLK:]
    near_kv = jnp.stack([upper_tile, upper_tile, lower_tile, lower_tile], 1).reshape(
        2, nblock, BLK, head_count, HEAD_WIDTH
    )
    group_tile = coarsen(level_one)
    far_tiles = []
    for level_num in range(2, LEV + 1):
        partner = partner_2(group_tile, "seq", level_num - 2)
        far_tiles.append(partner)
        if level_num < LEV:
            upper_half = seq_index >> level_num - 2 & 1 == 1
            joined = jnp.where(
                upper_half,
                jnp.concatenate([partner, group_tile], 1),
                jnp.concatenate([group_tile, partner], 1),
            )
            group_tile = coarsen(joined)
    far_kv = jnp.concatenate(far_tiles, 1).reshape(2, (LEV - 1) * BLK, head_count, HEAD_WIDTH)
    block_ids = seq_index * nblock + jnp.arange(nblock)
    total_blocks = seq_count * nblock
    band_valid = jnp.stack(
        [
            (block_ids + offset - 1 >= 0) & (block_ids + offset - 1 < total_blocks)
            for offset in range(3)
        ],
        1,
    )
    valid_mask = jnp.concatenate(
        [jnp.repeat(band_valid, BLK, axis=1), jnp.ones((nblock, LEV * BLK), bool)], 1
    )
    level_bias = jnp.concatenate(
        [
            jnp.zeros((3 * BLK,), jnp.float32),
            jnp.repeat(LOG_TWO * jnp.arange(1, LEV + 1).astype(jnp.float32), BLK),
        ]
    )
    qblocks = queries.reshape(nblock, BLK, head_count, HEAD_WIDTH)
    unscaled_scores = jnp.concatenate(
        [
            jnp.einsum("bqhd,bkhd->bhqk", qblocks, band_kv[0], preferred_element_type=jnp.float32),
            jnp.einsum("bqhd,bkhd->bhqk", qblocks, near_kv[0], preferred_element_type=jnp.float32),
            jnp.einsum("bqhd,khd->bhqk", qblocks, far_kv[0], preferred_element_type=jnp.float32),
        ],
        -1,
    )
    scores = jnp.where(
        valid_mask[:, None, None, :], unscaled_scores * score_scale + level_bias, -jnp.inf
    )
    row_max = jnp.max(scores, -1, keepdims=True)
    exp_terms = jnp.exp(scores - row_max)
    probs = exp_terms / jnp.sum(exp_terms, -1, keepdims=True)
    lower_probabilities = probs.astype(jnp.bfloat16)
    blended_output = jnp.einsum(
        "bhqk,bkhd->bqhd",
        lower_probabilities[..., :edge_cols],
        band_kv[1],
        preferred_element_type=jnp.float32,
    )
    blended_output = blended_output + jnp.einsum(
        "bhqk,bkhd->bqhd",
        lower_probabilities[..., edge_cols:middle_cols],
        near_kv[1],
        preferred_element_type=jnp.float32,
    )
    blended_output = blended_output + jnp.einsum(
        "bhqk,khd->bqhd",
        lower_probabilities[..., middle_cols:],
        far_kv[1],
        preferred_element_type=jnp.float32,
    )
    attended = blended_output.astype(jnp.bfloat16).reshape(row_count, col_count)
    attended_wide = attended.astype(jnp.float32)
    gain_wide = gain.astype(jnp.float32)
    scaled_grad = upstream.astype(jnp.float32) * gain_wide
    square_sum, projection = lax.psum(
        (jnp.sum(attended_wide * attended_wide, -1), jnp.sum(scaled_grad * attended_wide, -1)),
        "head",
    )
    columns = col_count * lax.axis_size("head")
    inv_rms = lax.rsqrt(square_sum / columns + EPSILON)[:, None]
    normed = (attended_wide * inv_rms * gain_wide).astype(jnp.bfloat16)
    d_attended = (
        inv_rms * scaled_grad
        - attended_wide * (inv_rms * inv_rms * inv_rms) * projection[:, None] / columns
    ).astype(jnp.bfloat16)
    block_gradients = d_attended.reshape(nblock, BLK, head_count, HEAD_WIDTH)
    probability_gradient = jnp.concatenate(
        [
            jnp.einsum(
                "bqhd,bkhd->bhqk", block_gradients, band_kv[1], preferred_element_type=jnp.float32
            ),
            jnp.einsum(
                "bqhd,bkhd->bhqk", block_gradients, near_kv[1], preferred_element_type=jnp.float32
            ),
            jnp.einsum(
                "bqhd,khd->bhqk", block_gradients, far_kv[1], preferred_element_type=jnp.float32
            ),
        ],
        -1,
    )
    inner_sum = jnp.sum(probs * probability_gradient, -1, keepdims=True)
    score_gradient = (probs * (probability_gradient - inner_sum) * score_scale).astype(jnp.bfloat16)
    grad_mixed = jnp.einsum(
        "bhqk,bkhd->bqhd",
        score_gradient[..., :edge_cols],
        band_kv[0],
        preferred_element_type=jnp.float32,
    )
    grad_mixed = grad_mixed + jnp.einsum(
        "bhqk,bkhd->bqhd",
        score_gradient[..., edge_cols:middle_cols],
        near_kv[0],
        preferred_element_type=jnp.float32,
    )
    grad_mixed = grad_mixed + jnp.einsum(
        "bhqk,khd->bqhd",
        score_gradient[..., middle_cols:],
        far_kv[0],
        preferred_element_type=jnp.float32,
    )
    grad_queries = grad_mixed.astype(jnp.bfloat16).reshape(row_count, col_count)
    band_grad = jnp.stack(
        [
            jnp.einsum(
                "bhqk,bqhd->bkhd",
                score_gradient[..., :edge_cols],
                qblocks,
                preferred_element_type=jnp.float32,
            ),
            jnp.einsum(
                "bhqk,bqhd->bkhd",
                lower_probabilities[..., :edge_cols],
                block_gradients,
                preferred_element_type=jnp.float32,
            ),
        ],
        0,
    )
    band_grad = band_grad.reshape(2, nblock, 3, BLK, col_count)
    summed_band = jnp.zeros((2, row_count + 2 * BLK, col_count), jnp.float32)
    for offset in range(3):
        placed = band_grad[:, :, offset].reshape(2, row_count, col_count)
        summed_band = summed_band + jnp.pad(
            placed, ((0, 0), (offset * BLK, (2 - offset) * BLK), (0, 0))
        )
    rim_terms = jnp.concatenate([summed_band[:, :BLK], summed_band[:, row_count + BLK :]], 1)
    arrived = padded_2(rim_terms, (("seq", 1),), BLK)
    interior = summed_band[:, BLK : row_count + BLK]
    interior = interior.at[:, :BLK].add(arrived[:, :BLK])
    interior = interior.at[:, row_count - BLK :].add(arrived[:, 3 * BLK :])
    near_grad = jnp.stack(
        [
            jnp.einsum(
                "bhqk,bqhd->bkhd",
                score_gradient[..., edge_cols:middle_cols],
                qblocks,
                preferred_element_type=jnp.float32,
            ),
            jnp.einsum(
                "bhqk,bqhd->bkhd",
                lower_probabilities[..., edge_cols:middle_cols],
                block_gradients,
                preferred_element_type=jnp.float32,
            ),
        ],
        0,
    )
    near_grad = near_grad.reshape(2, nblock, BLK, col_count)
    level_one_grad = jnp.concatenate(
        [near_grad[:, 2] + near_grad[:, 3], near_grad[:, 0] + near_grad[:, 1]], 1
    )
    far_grad = jnp.stack(
        [
            jnp.einsum(
                "bhqk,bqhd->khd",
                score_gradient[..., middle_cols:],
                qblocks,
                preferred_element_type=jnp.float32,
            ),
            jnp.einsum(
                "bhqk,bqhd->khd",
                lower_probabilities[..., middle_cols:],
                block_gradients,
                preferred_element_type=jnp.float32,
            ),
        ],
        0,
    )
    far_grad = far_grad.reshape(2, LEV - 1, BLK, col_count)
    half_rows = BLK // 2
    carried = None
    for level_num in range(LEV, 1, -1):
        arrived_tile = partner_2(far_grad[:, level_num - 2], "seq", level_num - 2)
        carried = arrived_tile if carried is None else carried + arrived_tile
        if level_num > 2:
            upper_half = seq_index >> level_num - 3 & 1 == 1
            kept_half = jnp.where(upper_half, carried[:, half_rows:], carried[:, :half_rows])
            sent_half = jnp.where(upper_half, carried[:, :half_rows], carried[:, half_rows:])
            carried = spread(kept_half + partner_2(sent_half, "seq", level_num - 3))
    level_zero = spread(spread(carried) + level_one_grad)
    total_grad = interior + level_zero
    return (
        normed,
        grad_queries,
        total_grad[0].astype(jnp.bfloat16),
        total_grad[1].astype(jnp.bfloat16),
    )


def solution(mesh):
    return jax.shard_map(
        body,
        mesh=mesh,
        in_specs=(
            P("seq", "head"),
            P("seq", "head"),
            P("seq", "head"),
            P("head"),
            P("seq", "head"),
        ),
        out_specs=(P("seq", "head"), P("seq", "head"), P("seq", "head"), P("seq", "head")),
        check_vma=False,
    )
```

profile of v0, /device:TPU:13, one launch (start us, length us, event | category | flops | bytes accessed | tf_op | source)
XLA Modules:
  0.0 593.1 jit_solution(9868038775790174930)
XLA Ops:
  11.9 4.7 maximum_convert_fusion
  16.6 11.2 %convert_reduce_fusion = (f32[2,128,2560]{2,1,0:T(8,128)}, bf16[2,128,1,2560]{3,2,1,0:T(2,128)(2,1)}) fusion(f32[2,128,2,2560]{3,2,1,0:T(2,128)S(1)} %maximum_convert_fusion), kind=kLoop, calls=%fused_computation.53 | loop fusion | flops 2621440 | bytes 9175040 | tf_op jit(solution)/shard_map/convert_element_type | solution.py:34
  32.1 4.8 fusion.110
  68.8 4.8 fusion.109
  80.8 9.4 %collective-permute-done.3 = bf16[2,64,2560]{2,1,0:T(8,128)(2,1)S(1)} collective-permute-done((bf16[2,64,2560]{2,1,0:T(8,128)(2,1)S(1)}, bf16[2,64,2560]{2,1,0:T(8,128)(2,1)S(1)}, u32[]{:S(2)}, u32[]{:S(2)}) %collective-permute-start.3) | collective-permute-done | bytes 655392 | tf_op jit(solution)/shard_map/ppermute | solution.py:29
  94.1 7.6 %squeeze.20 = bf16[4,192,20,128]{3,2,1,0:T(8,128)(2,1)} reshape(bf16[1,4,3,64,2560]{4,3,2,1,0:T(8,128)(2,1)} %get-tuple-element.37) | data formatting | bytes 7864320 | tf_op jit(solution)/shard_map/squeeze | solution.py:118
  101.7 7.6 %squeeze.21 = bf16[4,192,20,128]{3,2,1,0:T(8,128)(2,1)} reshape(bf16[1,4,3,64,2560]{4,3,2,1,0:T(8,128)(2,1)} %get-tuple-element.38) | data formatting | bytes 7864320 | tf_op jit(solution)/shard_map/squeeze | solution.py:102
  109.4 7.3 %fusion.33 = f32[4,20,64,192]{3,2,1,0:T(8,128)} fusion(bf16[4,192,20,128]{3,2,1,0:T(8,128)(2,1)} %squeeze.21, bf16[4,64,20,128]{3,2,1,0:T(8,128)(2,1)S(1)} %reshape.250), kind=kOutput, calls=%fused_computation.57 | convolution fusion | flops 251658240 | bytes 9175040 | tf_op jit(solution)/shard_map/bqhd,bkhd->bhqk/dot_general | solution.py:102
  118.5 14.4 %reshape.257 = f32[2,64,2,2560]{3,2,1,0:T(2,128)} reshape(f32[2,128,2560]{2,1,0:T(8,128)} %fusion.54) | data formatting | bytes 5242880 | tf_op jit(solution)/shard_map/convert_element_type | solution.py:34
  132.9 4.8 fusion.107
  140.5 27.3 %collective-permute-done.5 = bf16[2,64,2560]{2,1,0:T(8,128)(2,1)S(1)} collective-permute-done((bf16[2,64,2560]{2,1,0:T(8,128)(2,1)S(1)}, bf16[2,64,2560]{2,1,0:T(8,128)(2,1)S(1)}, u32[]{:S(2)}, u32[]{:S(2)}) %collective-permute-start.5) | collective-permute-done | bytes 655392 | tf_op jit(solution)/shard_map/ppermute | solution.py:29
  176.4 29.4 %fusion.111 = (f32[4,20,64]{2,0,1:T(4,128)S(1)}, f32[4,20,64,512]{3,2,0,1:T(8,128)S(1)}) fusion(f32[4,20,64,256]{3,2,0,1:T(8,128)S(1)} %bitcast.208, f32[512]{0:T(512)S(1)} %copy-done.36, pred[4,512]{1,0:T(4,128)(4,1)S(1)} %copy-done.35, f32[4,20,64,192]{3,2,1,0:T(8,128)} %fusion.33, f32[4,20,64,64]{3,2,1,0:T(8,128)} %convolution_bitcast_fusion.6), kind=kOutput, calls=%fused_computation.181 | output fusion | flops 18350592 | bytes 20996096 | tf_op jit(solution)/shard_map/sub | solution.py:112
  224.8 5.2 fusion.22
  233.1 7.4 %fusion.9 = f32[4,20,64,192]{3,2,0,1:T(8,128)} fusion(bf16[4,64,20,128]{3,1,0,2:T(8,128)(2,1)S(1)} %copy.189, bf16[4,192,20,128]{3,2,1,0:T(8,128)(2,1)} %squeeze.20), kind=kOutput, calls=%fused_computation.15 | convolution fusion | flops 251658240 | bytes 9175040 | tf_op jit(solution)/shard_map/bqhd,bkhd->bhqk/dot_general | solution.py:151
  247.9 58.9 %multiply_convert_fusion = bf16[4,20,64,512]{3,2,0,1:T(8,128)(2,1)S(1)} fusion(f32[4,20,64,256]{3,2,0,1:T(8,128)} %bitcast.209, f32[4,20,64,64]{3,2,0,1:T(8,128)S(1)} %fusion.63, f32[4,20,64,192]{3,2,0,1:T(8,128)} %fusion.9, f32[4,20,64,512]{3,2,0,1:T(8,128)} %copy-done.20, f32[4,20,64]{2,0,1:T(4,128)S(1)} %get-tuple-element.67), kind=kOutput, calls=%fused_computation.6 | output fusion | flops 28841472 | bytes 26234880 | tf_op jit(solution)/shard_map/sub | solution.py:164
  306.8 7.3 %fusion.13 = f32[4,20,128,64]{2,3,1,0:T(8,128)} fusion(bf16[4,192,20,128]{3,2,1,0:T(8,128)(2,1)} %squeeze.21, bf16[4,20,64,512]{3,2,0,1:T(8,128)(2,1)S(1)} %multiply_convert_fusion), kind=kOutput, calls=%fused_computation.19 | convolution fusion | flops 251658240 | bytes 9175040 | tf_op jit(solution)/shard_map/bhqk,bkhd->bqhd/dot_general | solution.py:165
  321.4 4.4 convolution_bitcast_fusion.1
  325.8 8.3 %copy.166 = f32[4,192,20,128]{3,2,1,0:T(8,128)} copy(f32[4,192,20,128]{3,1,2,0:T(8,128)S(1)} %convolution_bitcast_fusion) | data formatting | bytes 15728640 | tf_op jit(solution)/shard_map/bhqk,bqhd->bkhd/transpose | solution.py:192
  334.1 9.4 %stack.83 = f32[1,4,3,64,2560]{4,3,2,1,0:T(8,128)} reshape(f32[4,192,20,128]{3,2,1,0:T(8,128)} %copy.166) | data formatting | bytes 15728640 | tf_op jit(solution)/shard_map/stack | solution.py:184
  343.5 11.5 %copy.163 = f32[4,192,20,128]{3,2,1,0:T(8,128)} copy(f32[4,192,20,128]{3,1,2,0:T(8,128)} %convolution_bitcast_fusion.1) | data formatting | bytes 15728640 | tf_op jit(solution)/shard_map/bhqk,bqhd->bkhd/transpose | solution.py:186
  355.0 9.3 %stack.82 = f32[1,4,3,64,2560]{4,3,2,1,0:T(8,128)} reshape(f32[4,192,20,128]{3,2,1,0:T(8,128)} %copy.163) | data formatting | bytes 15728640 | tf_op jit(solution)/shard_map/stack | solution.py:184
  364.3 7.2 %constant_dynamic-update-slice_fusion.5 = f32[2,4,3,64,2560]{4,3,2,1,0:T(8,128)} fusion(f32[1,4,3,64,2560]{4,3,2,1,0:T(8,128)} %stack.82), kind=kLoop, calls=%fused_computation.146 | loop fusion | bytes 15728640
  375.5 11.4 %fusion.103 = (f32[2,4,1,64,2560]{4,3,2,1,0:T(8,128)}, f32[2,4,1,64,2560]{4,3,2,1,0:T(8,128)}, f32[2,4,1,64,2560]{4,3,2,1,0:T(8,128)}) fusion(f32[2,4,3,64,2560]{4,3,2,1,0:T(8,128)} %constant_dynamic-update-slice_fusion.4), kind=kLoop, calls=%fused_computation.173 | loop fusion | bytes 31457280 | tf_op jit(solution)/shard_map/slice | solution.py:204
  405.4 4.9 copy.168
  434.1 4.6 fusion.26
  456.4 23.4 %collective-permute-done.8 = f32[2,64,2560]{2,1,0:T(8,128)} collective-permute-done((f32[2,64,2560]{2,1,0:T(8,128)}, f32[2,64,2560]{2,1,0:T(8,128)}, u32[]{:S(2)}, u32[]{:S(2)}) %collective-permute-start.8) | collective-permute-done | bytes 1310752 | tf_op jit(solution)/shard_map/ppermute | solution.py:29
  484.9 37.1 %collective-permute-done.9 = f32[2,32,2560]{2,1,0:T(8,128)S(1)} collective-permute-done((f32[2,32,2560]{2,1,0:T(8,128)S(1)}, f32[2,32,2560]{2,1,0:T(8,128)S(1)}, u32[]{:S(2)}, u32[]{:S(2)}) %collective-permute-start.9) | collective-permute-done | bytes 655392 | tf_op jit(solution)/shard_map/ppermute | solution.py:29
  529.4 11.5 %collective-permute-done.6 = f32[2,64,2560]{2,1,0:T(8,128)S(1)} collective-permute-done((f32[2,64,2560]{2,1,0:T(8,128)S(1)}, f32[2,64,2560]{2,1,0:T(8,128)S(1)}, u32[]{:S(2)}, u32[]{:S(2)}) %collective-permute-start.6) | collective-permute-done | bytes 1310752 | tf_op jit(solution)/shard_map/ppermute | solution.py:20
  541.2 8.7 %collective-permute-done.11 = f32[2,32,2560]{2,1,0:T(8,128)S(1)} collective-permute-done((f32[2,32,2560]{2,1,0:T(8,128)S(1)}, f32[2,32,2560]{2,1,0:T(8,128)S(1)}, u32[]{:S(2)}, u32[]{:S(2)}) %collective-permute-start.11) | collective-permute-done | bytes 655392 | tf_op jit(solution)/shard_map/ppermute | solution.py:29
  551.3 13.5 %collective-permute-start.13 = (f32[2,32,2560]{2,1,0:T(8,128)S(1)}, f32[2,32,2560]{2,1,0:T(8,128)S(1)}, u32[]{:S(2)}, u32[]{:S(2)}) collective-permute-start(f32[2,32,2560]{2,1,0:T(8,128)S(1)} %slice_select_fusion), channel_id=1, source_target_pairs={{0,2},{2,0},{4,6},{6,4},{8,10},{10,8},{12,14},{14,12},{16,18},{18,... | collective-permute-start | bytes 1966088 | tf_op jit(solution)/shard_map/ppermute | solution.py:29
  578.7 7.6 %mul.172 = f32[2,256,2560]{2,1,0:T(8,128)} reshape(f32[2,128,2,2560]{3,2,1,0:T(2,128)} %broadcast_in_dim.52) | data formatting | bytes 10485760 | tf_op jit(solution)/shard_map/mul | solution.py:39
  586.3 4.8 add_convert_fusion
  (234 shorter events, 201.7 us)
Async XLA Ops:
  0.6 8.2 %copy-start.9 = (bf16[256,2560]{1,0:T(8,128)(2,1)S(1)}, bf16[256,2560]{1,0:T(8,128)(2,1)}, u32[]{:S(2)}) copy-start(bf16[256,2560]{1,0:T(8,128)(2,1)} %param.10) | copy-start | bytes 3932164
  0.6 9.6 %copy-start.8 = (bf16[256,2560]{1,0:T(8,128)(2,1)S(1)}, bf16[256,2560]{1,0:T(8,128)(2,1)}, u32[]{:S(2)}) copy-start(bf16[256,2560]{1,0:T(8,128)(2,1)} %param.11) | copy-start | bytes 3932164
  3.3 70.8 %collective-permute-start = (bf16[2,64,2560]{2,1,0:T(8,128)(2,1)}, bf16[2,64,2560]{2,1,0:T(8,128)(2,1)}, u32[]{:S(2)}, u32[]{:S(2)}) collective-permute-start(bf16[2,64,2560]{2,1,0:T(8,128)(2,1)} %get-tuple-element.51), channel_id=1, source_target_pairs={{0,2},{2,4},{4,6},{6,8},{8,10},{10,12},{12,14},{14,16},{16,18},{18... | collective-permute-start | bytes 1966088 | tf_op jit(solution)/shard_map/ppermute | solution.py:20
  6.9 67.2 %collective-permute-start.1 = (bf16[2,64,2560]{2,1,0:T(8,128)(2,1)}, bf16[2,64,2560]{2,1,0:T(8,128)(2,1)}, u32[]{:S(2)}, u32[]{:S(2)}) collective-permute-start(bf16[2,64,2560]{2,1,0:T(8,128)(2,1)} %get-tuple-element.52), channel_id=1, source_target_pairs={{2,0},{4,2},{6,4},{8,6},{10,8},{12,10},{14,12},{16,14},{18,16},{20... | collective-permute-start | bytes 1966088 | tf_op jit(solution)/shard_map/ppermute | solution.py:23
  37.9 23.3 %collective-permute-start.2 = (bf16[2,64,2560]{2,1,0:T(8,128)(2,1)}, bf16[2,64,2560]{2,1,0:T(8,128)(2,1)S(1)}, u32[]{:S(2)}, u32[]{:S(2)}) collective-permute-start(bf16[2,64,2560]{2,1,0:T(8,128)(2,1)} %fusion.77), channel_id=1, source_target_pairs={{0,2},{2,0},{4,6},{6,4},{8,10},{10,8},{12,14},{14,12},{16,18},{18,... | collective-permute-start | bytes 1966088 | tf_op jit(solution)/shard_map/ppermute | solution.py:29
  73.7 16.4 %collective-permute-start.3 = (bf16[2,64,2560]{2,1,0:T(8,128)(2,1)S(1)}, bf16[2,64,2560]{2,1,0:T(8,128)(2,1)S(1)}, u32[]{:S(2)}, u32[]{:S(2)}) collective-permute-start(bf16[2,64,2560]{2,1,0:T(8,128)(2,1)S(1)} %fusion.78), channel_id=1, source_target_pairs={{0,4},{2,6},{4,0},{6,2},{8,12},{10,14},{12,8},{14,10},{16,20},{18,... | collective-permute-start | bytes 1966088 | tf_op jit(solution)/shard_map/ppermute | solution.py:29
  93.1 23.5 %collective-permute-start.4 = (bf16[2,64,2560]{2,1,0:T(8,128)(2,1)S(1)}, bf16[2,64,2560]{2,1,0:T(8,128)(2,1)S(1)}, u32[]{:S(2)}, u32[]{:S(2)}) collective-permute-start(bf16[2,64,2560]{2,1,0:T(8,128)(2,1)S(1)} %fusion.79), channel_id=1, source_target_pairs={{0,8},{2,10},{4,12},{6,14},{8,0},{10,2},{12,4},{14,6},{16,24},{18,... | collective-permute-start | bytes 1966088 | tf_op jit(solution)/shard_map/ppermute | solution.py:29
  137.9 29.9 %collective-permute-start.5 = (bf16[2,64,2560]{2,1,0:T(8,128)(2,1)S(1)}, bf16[2,64,2560]{2,1,0:T(8,128)(2,1)S(1)}, u32[]{:S(2)}, u32[]{:S(2)}) collective-permute-start(bf16[2,64,2560]{2,1,0:T(8,128)(2,1)S(1)} %fusion.80), channel_id=1, source_target_pairs={{0,16},{2,18},{4,20},{6,22},{8,24},{10,26},{12,28},{14,30},{16,0},... | collective-permute-start | bytes 1966088 | tf_op jit(solution)/shard_map/ppermute | solution.py:29
  174.0 36.4 %slice-start.9 = ((s8[4718592]{0:T(1024)(128)(4,1)}), s8[4194304]{0:T(1024)(128)(4,1)S(1)}, s32[]{:S(2)}) async-start(s8[4718592]{0:T(1024)(128)(4,1)} %bitcast.195), calls=%async_computation.9 | async-start | bytes 8388608
  176.4 34.1 %slice-start.10 = ((s8[4718592]{0:T(1024)(128)(4,1)}), s8[524288]{0:T(1024)(128)(4,1)S(1)}, s32[]{:S(2)}) async-start(s8[4718592]{0:T(1024)(128)(4,1)} %bitcast.195), calls=%async_computation.10 | async-start | bytes 1048576
  232.7 8.6 %slice-start.6 = ((s8[5242880]{0:T(1024)(128)(4,1)}), s8[4194304]{0:T(1024)(128)(4,1)S(1)}, s32[]{:S(2)}) async-start(s8[5242880]{0:T(1024)(128)(4,1)} %bitcast.184), calls=%async_computation.6 | async-start | bytes 8388608
  233.1 7.5 %copy-start.18 = (bf16[4,64,20,128]{3,2,1,0:T(8,128)(2,1)S(1)}, bf16[4,64,20,128]{3,2,1,0:T(8,128)(2,1)}, u32[]{:S(2)}) copy-start(bf16[4,64,20,128]{3,2,1,0:T(8,128)(2,1)} %squeeze.24) | copy-start | bytes 3932164
  233.1 8.3 %slice-start.7 = ((s8[5242880]{0:T(1024)(128)(4,1)}), s8[1048576]{0:T(1024)(128)(4,1)S(1)}, s32[]{:S(2)}) async-start(s8[5242880]{0:T(1024)(128)(4,1)} %bitcast.184), calls=%async_computation.7 | async-start | bytes 2097152
  306.8 14.6 %copy-start.7 = (bf16[4,20,64,512]{3,2,0,1:T(8,128)(2,1)}, bf16[4,20,64,512]{3,2,0,1:T(8,128)(2,1)S(1)}, u32[]{:S(2)}) copy-start(bf16[4,20,64,512]{3,2,0,1:T(8,128)(2,1)S(1)} %multiply_convert_fusion) | copy-start | bytes 15728644
  306.8 7.3 %copy-start.16 = (bf16[4,64,20,128]{3,2,1,0:T(8,128)(2,1)S(1)}, bf16[4,64,20,128]{3,2,1,0:T(8,128)(2,1)}, u32[]{:S(2)}) copy-start(bf16[4,64,20,128]{3,2,1,0:T(8,128)(2,1)} %squeeze.22) | copy-start | bytes 3932164
  420.1 59.7 %collective-permute-start.8 = (f32[2,64,2560]{2,1,0:T(8,128)}, f32[2,64,2560]{2,1,0:T(8,128)}, u32[]{:S(2)}, u32[]{:S(2)}) collective-permute-start(f32[2,64,2560]{2,1,0:T(8,128)} %get-tuple-element.39), channel_id=1, source_target_pairs={{0,16},{2,18},{4,20},{6,22},{8,24},{10,26},{12,28},{14,30},{16,0},... | collective-permute-start | bytes 3932168 | tf_op jit(solution)/shard_map/ppermute | solution.py:29
  448.0 102.5 %collective-permute-start.12 = (f32[2,64,2560]{2,1,0:T(8,128)S(1)}, f32[2,64,2560]{2,1,0:T(8,128)S(1)}, u32[]{:S(2)}, u32[]{:S(2)}) collective-permute-start(f32[2,64,2560]{2,1,0:T(8,128)S(1)} %copy-done.32), channel_id=1, source_target_pairs={{0,4},{2,6},{4,0},{6,2},{8,12},{10,14},{12,8},{14,10},{16,20},{18,... | collective-permute-start | bytes 3932168 | tf_op jit(solution)/shard_map/ppermute | solution.py:29
  448.3 118.8 %collective-permute-start.14 = (f32[2,64,2560]{2,1,0:T(8,128)S(1)}, f32[2,64,2560]{2,1,0:T(8,128)S(1)}, u32[]{:S(2)}, u32[]{:S(2)}) collective-permute-start(f32[2,64,2560]{2,1,0:T(8,128)S(1)} %copy-done.31), channel_id=1, source_target_pairs={{0,2},{2,0},{4,6},{6,4},{8,10},{10,8},{12,14},{14,12},{16,18},{18,... | collective-permute-start | bytes 3932168 | tf_op jit(solution)/shard_map/ppermute | solution.py:29
  451.6 75.1 %collective-permute-start.10 = (f32[2,64,2560]{2,1,0:T(8,128)S(1)}, f32[2,64,2560]{2,1,0:T(8,128)S(1)}, u32[]{:S(2)}, u32[]{:S(2)}) collective-permute-start(f32[2,64,2560]{2,1,0:T(8,128)S(1)} %copy-done.33), channel_id=1, source_target_pairs={{0,8},{2,10},{4,12},{6,14},{8,0},{10,2},{12,4},{14,6},{16,24},{18,... | collective-permute-start | bytes 3932168 | tf_op jit(solution)/shard_map/ppermute | solution.py:29
  451.6 113.1 %collective-permute-start.7 = (f32[2,64,2560]{2,1,0:T(8,128)S(1)}, f32[2,64,2560]{2,1,0:T(8,128)S(1)}, u32[]{:S(2)}, u32[]{:S(2)}) collective-permute-start(f32[2,64,2560]{2,1,0:T(8,128)S(1)} %copy-done.29), channel_id=1, source_target_pairs={{2,0},{4,2},{6,4},{8,6},{10,8},{12,10},{14,12},{16,14},{18,16},{20... | collective-permute-start | bytes 3932168 | tf_op jit(solution)/shard_map/ppermute | solution.py:23
  454.0 86.8 %slice-start.4 = ((s8[5242880]{0:T(1024)(128)(4,1)}), s8[4194304]{0:T(1024)(128)(4,1)S(1)}, s32[]{:S(2)}) async-start(s8[5242880]{0:T(1024)(128)(4,1)} %bitcast.181), calls=%async_computation.4 | async-start | bytes 8388608
  455.2 85.7 %slice-start.5 = ((s8[5242880]{0:T(1024)(128)(4,1)}), s8[1048576]{0:T(1024)(128)(4,1)S(1)}, s32[]{:S(2)}) async-start(s8[5242880]{0:T(1024)(128)(4,1)} %bitcast.181), calls=%async_computation.5 | async-start | bytes 2097152
  456.4 65.6 %copy-start.30 = (f32[2,64,2560]{2,1,0:T(8,128)S(1)}, f32[2,64,2560]{2,1,0:T(8,128)}, u32[]{:S(2)}) copy-start(f32[2,64,2560]{2,1,0:T(8,128)} %get-tuple-element.33) | copy-start | bytes 3932164
  479.8 61.1 %slice-start.2 = ((s8[5242880]{0:T(1024)(128)(4,1)}), s8[4194304]{0:T(1024)(128)(4,1)S(1)}, s32[]{:S(2)}) async-start(s8[5242880]{0:T(1024)(128)(4,1)} %bitcast.176), calls=%async_computation.2 | async-start | bytes 8388608
  481.3 40.6 %collective-permute-start.9 = (f32[2,32,2560]{2,1,0:T(8,128)S(1)}, f32[2,32,2560]{2,1,0:T(8,128)S(1)}, u32[]{:S(2)}, u32[]{:S(2)}) collective-permute-start(f32[2,32,2560]{2,1,0:T(8,128)S(1)} %slice_select_fusion.2), channel_id=1, source_target_pairs={{0,8},{2,10},{4,12},{6,14},{8,0},{10,2},{12,4},{14,6},{16,24},{18,... | collective-permute-start | bytes 1966088 | tf_op jit(solution)/shard_map/ppermute | solution.py:29
  483.7 57.2 %slice-start = ((s8[5242880]{0:T(1024)(128)(4,1)}), s8[4194304]{0:T(1024)(128)(4,1)S(1)}, s32[]{:S(2)}) async-start(s8[5242880]{0:T(1024)(128)(4,1)} %bitcast.171), calls=%async_computation | async-start | bytes 8388608
  522.0 18.9 %collective-permute-start.6 = (f32[2,64,2560]{2,1,0:T(8,128)S(1)}, f32[2,64,2560]{2,1,0:T(8,128)S(1)}, u32[]{:S(2)}, u32[]{:S(2)}) collective-permute-start(f32[2,64,2560]{2,1,0:T(8,128)S(1)} %copy-done.30), channel_id=1, source_target_pairs={{0,2},{2,4},{4,6},{6,8},{8,10},{10,12},{12,14},{14,16},{16,18},{18... | collective-permute-start | bytes 3932168 | tf_op jit(solution)/shard_map/ppermute | solution.py:20
  526.2 14.7 %slice-start.3 = ((s8[5242880]{0:T(1024)(128)(4,1)}), s8[1048576]{0:T(1024)(128)(4,1)S(1)}, s32[]{:S(2)}) async-start(s8[5242880]{0:T(1024)(128)(4,1)} %bitcast.176), calls=%async_computation.3 | async-start | bytes 2097152
  526.7 14.2 %slice-start.1 = ((s8[5242880]{0:T(1024)(128)(4,1)}), s8[1048576]{0:T(1024)(128)(4,1)S(1)}, s32[]{:S(2)}) async-start(s8[5242880]{0:T(1024)(128)(4,1)} %bitcast.171), calls=%async_computation.1 | async-start | bytes 2097152
  527.1 13.9 %slice-start.8 = ((f32[2,384,2560]{2,1,0:T(8,128)}), f32[2,256,2560]{2,1,0:T(8,128)S(1)}, s32[]{:S(2)}) async-start(f32[2,384,2560]{2,1,0:T(8,128)} %pad_add_fusion), calls=%async_computation.8 | async-start | bytes 10485760 | tf_op jit(solution)/shard_map/slice | solution.py:210
  527.5 22.4 %collective-permute-start.11 = (f32[2,32,2560]{2,1,0:T(8,128)S(1)}, f32[2,32,2560]{2,1,0:T(8,128)S(1)}, u32[]{:S(2)}, u32[]{:S(2)}) collective-permute-start(f32[2,32,2560]{2,1,0:T(8,128)S(1)} %slice_select_fusion.1), channel_id=1, source_target_pairs={{0,4},{2,6},{4,0},{6,2},{8,12},{10,14},{12,8},{14,10},{16,20},{18,... | collective-permute-start | bytes 1966088 | tf_op jit(solution)/shard_map/ppermute | solution.py:29
  551.3 15.2 %collective-permute-start.13 = (f32[2,32,2560]{2,1,0:T(8,128)S(1)}, f32[2,32,2560]{2,1,0:T(8,128)S(1)}, u32[]{:S(2)}, u32[]{:S(2)}) collective-permute-start(f32[2,32,2560]{2,1,0:T(8,128)S(1)} %slice_select_fusion), channel_id=1, source_target_pairs={{0,2},{2,0},{4,6},{6,4},{8,10},{10,8},{12,14},{14,12},{16,18},{18,... | collective-permute-start | bytes 1966088 | tf_op jit(solution)/shard_map/ppermute | solution.py:29
  (33 other events, 118.5 us)
where the time goes:
time: 604 us; the launch traced here: 593 us
  local copies, waits for them, and re-layouts  224 us (37%)
  other arithmetic  146 us (24%)
  waiting for transfers between devices  119 us (20%)
  matrix products  58.8 us (10%)
  starting transfers between devices  39.7 us (7%)
    ppermute x11, waiting for transfers between devices, partner_2(): lax.ppermute(x, axis, [(i, i ^ 1 << bit) for i in range(lax.axis_size(axi...  107 us
    sub x1, other arithmetic, body(): probability_gradient - inner_sum  58.9 us
    sub x1, other arithmetic, body(): exp_terms = jnp.exp(scores - row_max)  29.4 us
    ppermute x11, starting transfers between devices, partner_2(): lax.ppermute(x, axis, [(i, i ^ 1 << bit) for i in range(lax.axis_size(axi...  29 us
    unnamed x106, local copies, waits for them, and re-layouts  28.6 us
    convert_element_type x4, local copies, waits for them, and re-layouts, coarsen(): tile.astype(jnp.float32)  25.2 us
    another operation x3, local copies, waits for them, and re-layouts, body(): jnp.stack([jnp.einsum('bhqk,bqhd->bkhd', score_gradient[..., :edge_cols],...  22.7 us
    convert_element_type x5, other arithmetic, coarsen(): tile.astype(jnp.float32)  21.1 us
  transfers between devices with their start and end apart: 15, of which 7 were waited for; matrix products, arithmetic and copies ran while one was open for 21% of the time, Pallas kernels for 0%

commit v1 on v0

v1 whole, which is shorter than its diff:
```python
import functools
import jax
import jax.numpy as jnp
from jax import lax
from jax.experimental import pallas as pl
from jax.experimental.pallas import tpu as pltpu
from jax.sharding import PartitionSpec as P

HEAD_WIDTH = 128
BLK = 64
LEV = 5
EPSILON = 1e-06
LOG2E = 1.4426950408889634
MESH = pl.DeviceIdType.MESH
HEADS_STEP = 4
FAR = tuple(1 << k for k in range(LEV - 1))
F32, BF16 = jnp.float32, jnp.bfloat16
NN = (((1,), (0,)), ((), ()))
NT = (((1,), (1,)), ((), ()))
TN = (((0,), (0,)), ((), ()))


def dot(a, b, dims):
    return lax.dot_general(a, b, dims, preferred_element_type=F32)


def piece_shapes(cols):
    return [(n, 2 * BLK // n, cols) for n in FAR]


def exchange(me, count, far_src, far_dst, edge_src, edge_dst, sems, prepare):
    send_far, recv_far, send_edge, recv_edge = sems
    barrier = pltpu.get_barrier_semaphore()
    peers = []
    for k, n in enumerate(FAR):
        g, o = me // n, me % n
        base = (g + 1 - 2 * (g % 2)) * n
        for r in range(n):
            peers.append((k, n, r, base + (o + r) % n, (o + r) % n, o))
    has = (me > 0, me < count - 1)
    ids = (me - 1, me + 1)
    for peer in peers:
        pl.semaphore_signal(barrier, inc=1, device_id={"seq": peer[3]}, device_id_type=MESH)
    for side in range(2):
        @pl.when(has[side])
        def _():
            pl.semaphore_signal(barrier, inc=1, device_id={"seq": ids[side]}, device_id_type=MESH)
    pl.semaphore_wait(
        barrier, len(peers) + has[0].astype(jnp.int32) + has[1].astype(jnp.int32))

    def edge_copy(side, part):
        return pltpu.make_async_remote_copy(
            src_ref=edge_src(side, part), dst_ref=edge_dst(1 - side, part),
            send_sem=send_edge.at[side, part], recv_sem=recv_edge.at[1 - side, part],
            device_id={"seq": ids[side]}, device_id_type=MESH)

    def edge_wait(side, part):
        return pltpu.make_async_remote_copy(
            src_ref=edge_src(side, part), dst_ref=edge_dst(side, part),
            send_sem=send_edge.at[side, part], recv_sem=recv_edge.at[side, part],
            device_id={"seq": ids[side]}, device_id_type=MESH)

    for side in range(2):
        @pl.when(has[side])
        def _():
            for part in range(2):
                edge_copy(side, part).start()
    prepare()
    copies = []
    for k, n, r, dest, t, o in reversed(peers):
        copies.append(pltpu.make_async_remote_copy(
            src_ref=far_src(k, t), dst_ref=far_dst(k, o),
            send_sem=send_far.at[n - 1 + r], recv_sem=recv_far.at[n - 1 + r],
            device_id={"seq": dest}, device_id_type=MESH))
        copies[-1].start()
    for copy in copies:
        copy.wait()
    for side in range(2):
        @pl.when(has[side])
        def _():
            for part in range(2):
                edge_wait(side, part).wait_send()
                edge_wait(side, part).wait_recv()


def sem_shapes():
    total = sum(FAR)
    return [pltpu.SemaphoreType.DMA((total,)), pltpu.SemaphoreType.DMA((total,)),
            pltpu.SemaphoreType.DMA((2, 2)), pltpu.SemaphoreType.DMA((2, 2))]


def halve(x):
    n = x.shape[0]
    row = lax.broadcasted_iota(jnp.int32, (n // 2, n), 0)
    col = lax.broadcasted_iota(jnp.int32, (n // 2, n), 1)
    mat = jnp.where((col == 2 * row) | (col == 2 * row + 1), 0.5, 0.0).astype(BF16)
    return dot(mat, x, NN)


def gather_kernel(count, k_ref, v_ref, l1_ref, r2, r3, r4, r5, edge_ref,
                  s2, s3, s4, s5, *sems):
    me = lax.axis_index("seq")
    rows, cols = k_ref.shape
    far_scr, far_out = (s2, s3, s4, s5), (r2, r3, r4, r5)
    width = 4 * HEAD_WIDTH

    def prepare():
        def step(i, _):
            c = pl.ds(pl.multiple_of(i * width, width), width)
            for part, ref in enumerate((k_ref, v_ref)):
                level = halve(ref[:, c]).astype(BF16)
                l1_ref[part, :, c] = level
                for scr, n in zip((s2, s3, s4), FAR):
                    level = halve(level).astype(BF16)
                    m = BLK // n
                    scr[part * m:(part + 1) * m, c] = level
            last = jnp.concatenate(
                [halve(s4[:16, c]), halve(s4[16:, c])], 0)
            s5[:, c] = last.astype(BF16)
            return 0
        lax.fori_loop(0, cols // width, step, 0)

    def edge_src(side, part):
        ref = (k_ref, v_ref)[part]
        return ref.at[pl.ds(0, BLK)] if side == 0 else ref.at[pl.ds(rows - BLK, BLK)]

    exchange(me, count, lambda k, t: far_scr[k], lambda k, o: far_out[k].at[o],
             edge_src, lambda side, part: edge_ref.at[side, part], sems, prepare)


def send_kernel(count, g2, g3, g4, g5, eg, r2, r3, r4, r5, er, *sems):
    me = lax.axis_index("seq")
    src, dst = (g2, g3, g4, g5), (r2, r3, r4, r5)
    exchange(me, count, lambda k, t: src[k].at[t], lambda k, o: dst[k].at[o],
             lambda side, part: eg.at[side, part], lambda side, part: er.at[side, part],
             sems, lambda: None)


def keep(x, flag):
    return jnp.where(flag, x.astype(F32), 0.0).astype(BF16)


def load_sets(me, count, c, k_ref, v_ref, l1_ref, far_refs, edge_ref):
    sets = []
    for part, ref in enumerate((k_ref, v_ref)):
        x = ref[:, c]
        low = keep(edge_ref[0, part, :, c], me > 0)
        high = keep(edge_ref[1, part, :, c], me < count - 1)
        far = []
        for n, far_ref in zip(FAR, far_refs):
            m = BLK // n
            if m >= 16:
                far.append(far_ref[:, part * m:(part + 1) * m, c].reshape(BLK, HEAD_WIDTH))
            else:
                wide = far_ref[:, :, c].astype(F32)
                far.append(wide[:, part * m:(part + 1) * m].reshape(BLK, HEAD_WIDTH).astype(BF16))
        sets.append((
            jnp.concatenate([low, x[:3 * BLK], l1_ref[part, BLK:, c]] + far, 0),
            jnp.concatenate([x[BLK:], high, l1_ref[part, :BLK, c]] + far, 0)))
    return sets


def forward_kernel(count, q_ref, k_ref, v_ref, u_ref, gain_ref, bias_ref, l1_ref,
                   r2, r3, r4, r5, edge_ref, att_ref, lse_ref, stat_ref):
    me = lax.axis_index("seq")

    @pl.when(pl.program_id(0) == 0)
    def _():
        stat_ref[...] = jnp.zeros_like(stat_ref)

    for h in range(HEADS_STEP):
        c = slice(h * HEAD_WIDTH, (h + 1) * HEAD_WIDTH)
        keys, values = load_sets(me, count, c, k_ref, v_ref, l1_ref, (r2, r3, r4, r5), edge_ref)
        gain = gain_ref[:, c].astype(F32)
        for p in range(2):
            rows = slice(p * 2 * BLK, (p + 1) * 2 * BLK)
            s = dot(keys[p], q_ref[rows, c], NT) * (LOG2E * HEAD_WIDTH ** -0.5) + bias_ref[p]
            top = jnp.max(s, 0, keepdims=True)
            e = jnp.exp2(s - top)
            total = jnp.sum(e, 0, keepdims=True)
            low = (e * (1.0 / total)).astype(BF16)
            lse_ref[h, :, rows] = top + jnp.log2(total)
            att = dot(low, values[p], TN).astype(BF16)
            att_ref[rows, c] = att
            wide = att.astype(F32)
            sg = u_ref[rows, c].astype(F32) * gain
            stat_ref[0, rows, :] += wide * wide
            stat_ref[1, rows, :] += sg * wide


def backward_kernel(count, q_ref, k_ref, v_ref, u_ref, gain_ref, bias_ref, l1_ref,
                    r2, r3, r4, r5, edge_ref, att_ref, lse_ref, coef_ref,
                    norm_ref, gq_ref, loc_ref, gl1_ref, g2, g3, g4, g5, eg_ref):
    me = lax.axis_index("seq")
    scale = HEAD_WIDTH ** -0.5
    for h in range(HEADS_STEP):
        c = slice(h * HEAD_WIDTH, (h + 1) * HEAD_WIDTH)
        keys, values = load_sets(me, count, c, k_ref, v_ref, l1_ref, (r2, r3, r4, r5), edge_ref)
        gain = gain_ref[:, c].astype(F32)
        terms = []
        for p in range(2):
            rows = slice(p * 2 * BLK, (p + 1) * 2 * BLK)
            q = q_ref[rows, c]
            inv, back = coef_ref[rows, 0:1], coef_ref[rows, 1:2]
            wide = att_ref[rows, c].astype(F32)
            sg = u_ref[rows, c].astype(F32) * gain
            norm_ref[rows, c] = (wide * inv * gain).astype(BF16)
            d = (inv * sg - wide * back).astype(BF16)
            s = dot(keys[p], q, NT) * (LOG2E * scale) + bias_ref[p]
            probs = jnp.exp2(s - lse_ref[h, :, rows])
            dp = dot(values[p], d, NT)
            inner = jnp.sum(probs * dp, 0, keepdims=True)
            ds = (probs * (dp - inner) * scale).astype(BF16)
            gq_ref[rows, c] = dot(ds, keys[p], TN).astype(BF16)
            terms.append((dot(ds, q, NN), dot(probs.astype(BF16), d, NN)))
        for part in range(2):
            a, b = terms[0][part], terms[1][part]
            eg_ref[0, part, :, c] = a[:BLK].astype(BF16)
            eg_ref[1, part, :, c] = b[3 * BLK:4 * BLK].astype(BF16)
            loc_ref[part, :, c] = jnp.concatenate(
                [a[BLK:2 * BLK], a[2 * BLK:4 * BLK] + b[:2 * BLK], b[2 * BLK:3 * BLK]], 0)
            gl1_ref[part, :, c] = jnp.concatenate(
                [b[4 * BLK:5 * BLK], a[4 * BLK:5 * BLK]], 0).astype(BF16)
        both = [terms[0][part][5 * BLK:] + terms[1][part][5 * BLK:] for part in range(2)]
        for k, (n, g) in enumerate(zip(FAR, (g2, g3, g4, g5))):
            m = BLK // n
            parts = [x[k * BLK:(k + 1) * BLK].reshape(n, m, HEAD_WIDTH) for x in both]
            g[:, :, c] = jnp.concatenate(parts, 1).astype(BF16)


def combine_kernel(count, loc_ref, gl1_ref, r2, r3, r4, r5, er_ref, gk_ref, gv_ref):
    me = lax.axis_index("seq")
    row_count, span = gk_ref.shape
    flags = (me > 0, me < count - 1)
    row = lax.broadcasted_iota(jnp.int32, (row_count, 2 * BLK + 4 * BLK), 0)
    col = lax.broadcasted_iota(jnp.int32, (row_count, 2 * BLK + 4 * BLK), 1)
    mat = jnp.where((col < 2 * BLK) & (row // 2 == col), 0.5, 0.0)
    for k, n in enumerate(FAR):
        first = (2 + k) * BLK
        m = BLK // n
        inside = (col >= first) & (col < first + BLK)
        mat += jnp.where(inside & (row // (4 * n) == (col - first) % m), 0.25 / n, 0.0)
    mat = mat.astype(BF16)
    for part, out in enumerate((gk_ref, gv_ref)):
        far = [gl1_ref[part]]
        for n, ref in zip(FAR, (r2, r3, r4, r5)):
            m = BLK // n
            if m >= 16:
                far.append(ref[:, part * m:(part + 1) * m, :].reshape(BLK, span))
            else:
                wide = ref[...].astype(F32)
                far.append(wide[:, part * m:(part + 1) * m].reshape(BLK, span).astype(BF16))
        total = loc_ref[part] + dot(mat, jnp.concatenate(far, 0), NN)
        low = jnp.where(flags[0], er_ref[0, part].astype(F32), 0.0)
        high = jnp.where(flags[1], er_ref[1, part].astype(F32), 0.0)
        out[:BLK] = (total[:BLK] + low).astype(BF16)
        out[BLK:row_count - BLK] = total[BLK:row_count - BLK].astype(BF16)
        out[row_count - BLK:] = (total[row_count - BLK:] + high).astype(BF16)


def score_bias(seq_index, seq_count):
    key = jnp.arange(4 * BLK)[None, :, None] // BLK
    query = jnp.arange(2 * BLK)[None, None, :] // BLK
    pair = jnp.arange(2)[:, None, None]
    block = seq_index * 4 + 2 * pair + key - 1
    valid = (key >= query) & (key <= query + 2) & (block >= 0) & (block < 4 * seq_count)
    band = jnp.where(valid, 0.0, -1e30).astype(F32)
    levels = jnp.repeat(jnp.arange(1, LEV + 1).astype(F32), BLK)[None, :, None]
    return jnp.concatenate([band, jnp.broadcast_to(levels, (2, LEV * BLK, 2 * BLK))], 1)


def body(queries, keys_in, values_in, gain, upstream):
    rows, cols = queries.shape
    heads = cols // HEAD_WIDTH
    me = lax.axis_index("seq")
    count = lax.axis_size("seq")
    shape = jax.ShapeDtypeStruct
    any_spec = pl.BlockSpec(memory_space=pl.ANY)
    vmem = pl.BlockSpec(memory_space=pltpu.VMEM)
    pieces = piece_shapes(cols)
    piece_out = [shape(s, BF16) for s in pieces]
    edge_out = shape((2, 2, BLK, cols), BF16)
    limit = 48 * 1024 * 1024

    l1, *recv = pl.pallas_call(
        functools.partial(gather_kernel, count),
        out_shape=[shape((2, rows // 2, cols), BF16)] + piece_out + [edge_out],
        in_specs=[vmem] * 2,
        out_specs=[vmem] + [any_spec] * 5,
        scratch_shapes=[pltpu.VMEM(s[1:], BF16) for s in pieces] + sem_shapes(),
        compiler_params=pltpu.CompilerParams(
            collective_id=0, has_side_effects=True, vmem_limit_bytes=limit),
        name="gather_tiles",
    )(keys_in, values_in)
    bias = score_bias(me, count)
    gain2 = gain.reshape(1, cols)

    step = HEADS_STEP * HEAD_WIDTH
    grid = (heads // HEADS_STEP,)
    flat = lambda n: pl.BlockSpec((n, step), lambda i: (0, i))
    cube = lambda a, b: pl.BlockSpec((a, b, step), lambda i: (0, 0, i))
    quad = pl.BlockSpec((2, 2, BLK, step), lambda i: (0, 0, 0, i))
    fixed = lambda s: pl.BlockSpec(s, lambda i: (0,) * len(s))
    piece_specs = [cube(s[0], s[1]) for s in pieces]
    lse_spec = pl.BlockSpec((HEADS_STEP, 1, rows), lambda i: (i, 0, 0))
    shared = [flat(rows)] * 4 + [flat(1), fixed(bias.shape), cube(2, rows // 2)] + piece_specs + [quad]
    params = pltpu.CompilerParams(vmem_limit_bytes=limit)
    common = (queries, keys_in, values_in, upstream, gain2, bias, l1, *recv)
    att, lse, stat = pl.pallas_call(
        functools.partial(forward_kernel, count),
        grid=grid,
        out_shape=[shape((rows, cols), BF16), shape((heads, 1, rows), F32),
                   shape((2, rows, HEAD_WIDTH), F32)],
        in_specs=shared,
        out_specs=[flat(rows), lse_spec, fixed((2, rows, HEAD_WIDTH))],
        compiler_params=params,
        name="attend",
    )(*common)

    sums = jnp.sum(stat, -1)
    parts = lax.axis_size("head")
    total = sums
    for shift in range(1, parts):
        total = total + lax.ppermute(
            sums, "head", [(i, (i + shift) % parts) for i in range(parts)])
    columns = cols * parts
    inv = lax.rsqrt(total[0] / columns + EPSILON)
    coef = jnp.stack([inv, inv * inv * inv * total[1] / columns], 1)

    normed, gq, loc, gl1, *grads = pl.pallas_call(
        functools.partial(backward_kernel, count),
        grid=grid,
        out_shape=[shape((rows, cols), BF16)] * 2
        + [shape((2, rows, cols), F32), shape((2, rows // 2, cols), BF16)]
        + piece_out + [edge_out],
        in_specs=shared + [flat(rows), lse_spec, fixed((rows, 2))],
        out_specs=[flat(rows)] * 2 + [cube(2, rows), cube(2, rows // 2)] + piece_specs + [quad],
        compiler_params=params,
        name="differentiate",
    )(*common, att, lse, coef)

    back = pl.pallas_call(
        functools.partial(send_kernel, count),
        out_shape=piece_out + [edge_out],
        in_specs=[any_spec] * 5,
        out_specs=[any_spec] * 5,
        scratch_shapes=sem_shapes(),
        compiler_params=pltpu.CompilerParams(
            collective_id=1, has_side_effects=True, vmem_limit_bytes=limit),
        name="send_terms",
    )(*grads)

    gk, gv = pl.pallas_call(
        functools.partial(combine_kernel, count),
        grid=grid,
        out_shape=[shape((rows, cols), BF16)] * 2,
        in_specs=[cube(2, rows), cube(2, rows // 2)] + piece_specs + [quad],
        out_specs=[flat(rows)] * 2,
        compiler_params=params,
        name="combine",
    )(loc, gl1, *back)
    return normed, gq, gk, gv


def solution(mesh):
    spec = P("seq", "head")
    return jax.shard_map(
        body,
        mesh=mesh,
        in_specs=(spec, spec, spec, P("head"), spec),
        out_specs=(spec,) * 4,
        check_vma=False,
    )
```

time: 604 us -> 152 us (0.25); the launches traced: 593 us -> 150 us
  local copies, waits for them, and re-layouts: 224 us -> 7.74 us
  other arithmetic: 146 us -> 0.71 us
  Pallas kernels: 0 us -> 138 us
  waiting for transfers between devices: 119 us -> 2.21 us
  matrix products: 58.8 us -> 0 us
  starting transfers between devices: 39.7 us -> 0.29 us
    pallas_call x0 -> x5, Pallas kernels: none -> 138 us  [the longest x1 48.7 us: body(): pl.pallas_call(functools.partial(gather_kernel, count), out_shape=[shape(...]
    ppermute x15 -> x1, waiting for transfers between devices: 119 us -> 2.21 us  [body(): lax.ppermute(sums, 'head', [(i, (i + shift) % parts) for i in range(parts)])]
    sub x2 -> x0, other arithmetic: 88.3 us -> none  [the longest x1 58.9 us: body(): probability_gradient - inner_sum]
    dot_general x16 -> x0, matrix products: 53.4 us -> none  [the longest x1 7.43 us: body(): jnp.einsum('bqhd,bkhd->bhqk', block_gradients, band_kv[1], preferred_elem...]
    another operation x12 -> x1, local copies, waits for them, and re-layouts: 40.2 us -> 0.14 us  [body(): coef = jnp.stack([inv, inv * inv * inv * total[1] / columns], 1)]
    ppermute x15 -> x1, starting transfers between devices: 39.7 us -> 0.29 us  [body(): lax.ppermute(sums, 'head', [(i, (i + shift) % parts) for i in range(parts)])]
    slice x12 -> x0, local copies, waits for them, and re-layouts: 37.2 us -> none  [the longest x4 14.5 us: coarsen(): return (0.5 * (pairs[..., 0, :] + pairs[..., 1, :])).astype(jnp.bfloat16)]
    transpose x6 -> x0, local copies, waits for them, and re-layouts: 32.8 us -> none  [the longest x1 11.5 us: body(): jnp.einsum('bhqk,bqhd->bkhd', score_gradient[..., :edge_cols], qblocks, p...]
  transfers between devices with their start and end apart: 15 -> 1, of which waited for: 7 -> 1; matrix products, arithmetic and copies ran while one was open for 21% -> 0% of each run, Pallas kernels for 0% -> 0%
where the time goes in v1:
time: 152 us; the launch traced here: 150 us
  Pallas kernels  138 us (91%)
  local copies, waits for them, and re-layouts  7.74 us (5%)
  waiting for transfers between devices  2.21 us (1%)
    pallas_call x1, Pallas kernels, body(): pl.pallas_call(functools.partial(gather_kernel, count), out_shape=[shape(...  48.7 us
    pallas_call x1, Pallas kernels, body(): pl.pallas_call(functools.partial(send_kernel, count), out_shape=piece_out...  46.7 us
    pallas_call x1, Pallas kernels, body(): pl.pallas_call(functools.partial(backward_kernel, count), grid=grid, out_...  22 us
    pallas_call x1, Pallas kernels, body(): pl.pallas_call(functools.partial(forward_kernel, count), grid=grid, out_s...  15.1 us
    unnamed x20, local copies, waits for them, and re-layouts  6.75 us
    pallas_call x1, Pallas kernels, body(): pl.pallas_call(functools.partial(combine_kernel, count), grid=grid, out_s...  6.03 us
  transfers between devices with their start and end apart: 1, of which 1 were waited for; matrix products, arithmetic and copies ran while one was open for 0% of the time, Pallas kernels for 0%

profile of v1, /device:TPU:13, one launch (start us, length us, event | category | flops | bytes accessed | tf_op | source)
XLA Modules:
  0.0 150.2 jit_solution(7527128907937572787)
XLA Ops:
  0.7 0.1 broadcast_in_dim.23
  0.8 0.1 reshape.247
  0.8 0.7 reshape.246.gain_ref
  1.5 0.1 fusion.1
  1.6 0.1 compare_and_fusion
  1.7 0.2 and_select_fusion
  1.9 0.1 pad_maximum_fusion.bias_ref
  2.1 0.0 copy-start
  2.1 48.7 %gather_tiles.1 = (bf16[2,128,2560]{2,1,0:T(8,128)(2,1)S(1)}, bf16[1,128,2560]{2,1,0:T(8,128)(2,1)S(1)}, bf16[2,64,2560]{2,1,0:T(8,128)(2,1)S(1)}, bf16[4,32,256...) custom-call(bf16[256,2560]{1,0:T(8,128)(2,1)} %k_ref.5, ...), custom_call_target="tpu_custom_call" | custom-call | tf_op jit(solution)/shard_map/gather_tiles/pallas_call | solution.py:285
  50.8 0.0 copy-start.1
  50.8 1.0 copy-done.1
  51.8 0.0 copy-start.2
  51.8 1.1 copy-done.2
  52.9 0.0 copy-done
  52.9 15.1 %attend.1 = (bf16[256,2560]{1,0:T(8,128)(2,1)S(1)}, f32[20,1,256]{2,1,0:T(1,128)S(1)}, f32[2,256,128]{2,1,0:T(8,128)S(1)}) custom-call(bf16[256,2560]{1,0:T(8,128)(2,1)S(1)} %copy-done, bf16[256,2560]{1,0:T(8,128)(2,1)} %k_ref.5, bf16[256,2560]{1,0:T(8,128)(2,1)} %v_ref.5, bf16[256,2560]{1,0:T(8,128)(2,1)} %u_ref.3, bf16[1,2560]{1,0:T(2,128)(2,1)S(1)} %reshape.246.gain_ref, ...), custom_call_target="tpu_custom_call" | custom-call | tf_op jit(solution)/shard_map/attend/pallas_call | solution.py:309
  68.0 0.0 copy-done.3
  68.0 0.0 copy-done.5
  68.0 0.0 copy-start.9
  68.0 1.1 copy-done.9
  69.1 0.1 reduce_sum.9
  69.3 0.3 collective-permute-start
  69.6 2.2 %collective-permute-done = f32[2,256]{1,0:T(2,128)S(1)} collective-permute-done((f32[2,256]{1,0:T(2,128)S(1)}, f32[2,256]{1,0:T(2,128)S(1)}, u32[]{:S(2)}, u32[]{:S(2)}) %collective-permute-start) | collective-permute-done | bytes 2080 | tf_op jit(solution)/shard_map/ppermute | solution.py:324
  71.8 0.1 copy.14.coef_ref
  72.0 0.0 copy-start.4
  72.0 1.1 copy-done.4
  73.1 1.1 copy-done.6
  74.1 22.0 %differentiate.1 = (bf16[256,2560]{1,0:T(8,128)(2,1)}, bf16[256,2560]{1,0:T(8,128)(2,1)}, f32[2,256,2560]{2,1,0:T(8,128)}, bf16[2,128,2560]{2,1,0:T(8,128)(2,1)}...) custom-call(bf16[256,2560]{1,0:T(8,128)(2,1)} %q_ref.3, ...), custom_call_target="tpu_custom_call" | custom-call | tf_op jit(solution)/shard_map/differentiate/pallas_call | solution.py:330
  96.2 46.7 %send_terms.1 = (bf16[1,128,2560]{2,1,0:T(8,128)(2,1)S(1)}, bf16[2,64,2560]{2,1,0:T(8,128)(2,1)S(1)}, bf16[4,32,2560]{2,1,0:T(8,128)(2,1)S(1)}, bf16[8,16,2560]{2,1,0:T(8,128)(2,1)S(1)}, bf16[2,2,64,2560]{3,2,1,0:T(8,128)(2,1)}) custom-call(bf16[1,128,2560]{2,1,0:T(8,128)(2,1)S(1)} %get-tuple-element.42.g2, bf16[2,64,2560]{2,1,0:T(8,128)(2,1)S(1)} %get-tuple-element.43.g3, ...), custom_call_target="tpu_custom_call" | custom-call | tf_op jit(solution)/shard_map/send_terms/pallas_call | solution.py:342
  142.9 0.0 copy-done.7
  142.9 0.0 copy-start.8
  142.9 1.3 copy-done.8
  144.2 6.0 %combine.1 = (bf16[256,2560]{1,0:T(8,128)(2,1)}, bf16[256,2560]{1,0:T(8,128)(2,1)}) custom-call(f32[2,256,2560]{2,1,0:T(8,128)} %get-tuple-element.40.loc_ref, bf16[2,128,2560]{2,1,0:T(8,128)(2,1)S(1)} %copy-done.7, bf16[1,128,2560]{2,1,0:T(8,128)(2,1)S(1)} %get-tuple-element.47.r2, bf16[2,64,2560]{2,1,0:T(8,128)(2,1)S(1)} %get-tuple-element.48.r3, ...), custom_call_target="tpu_custom_call" | custom-call | tf_op jit(solution)/shard_map/combine/pallas_call | solution.py:353
  (12 shorter events, 0.1 us)
Async XLA Ops:
  2.1 50.8 %copy-start = (bf16[256,2560]{1,0:T(8,128)(2,1)S(1)}, bf16[256,2560]{1,0:T(8,128)(2,1)}, u32[]{:S(2)}) copy-start(bf16[256,2560]{1,0:T(8,128)(2,1)} %q_ref.3) | copy-start | bytes 3932164
  50.8 1.1 copy-start.1
  51.8 1.1 copy-start.2
  52.9 15.1 %copy-start.3 = (bf16[4,32,2560]{2,1,0:T(8,128)(2,1)}, bf16[4,32,2560]{2,1,0:T(8,128)(2,1)S(1)}, u32[]{:S(2)}) copy-start(bf16[4,32,2560]{2,1,0:T(8,128)(2,1)S(1)} %get-tuple-element.32.r4) | copy-start | bytes 1966084
  52.9 15.1 %copy-start.5 = (bf16[8,16,2560]{2,1,0:T(8,128)(2,1)}, bf16[8,16,2560]{2,1,0:T(8,128)(2,1)S(1)}, u32[]{:S(2)}) copy-start(bf16[8,16,2560]{2,1,0:T(8,128)(2,1)S(1)} %get-tuple-element.33.r5) | copy-start | bytes 1966084
  68.0 1.1 copy-start.9
  69.3 2.5 %collective-permute-start = (f32[2,256]{1,0:T(2,128)S(1)}, f32[2,256]{1,0:T(2,128)S(1)}, u32[]{:S(2)}, u32[]{:S(2)}) collective-permute-start(f32[2,256]{1,0:T(2,128)S(1)} %reduce_sum.9), channel_id=1, source_target_pairs={{0,1},{1,0},{2,3},{3,2},{4,5},{5,4},{6,7},{7,6},{8,9},{9,8},{10,11... | collective-permute-start | bytes 6152 | tf_op jit(solution)/shard_map/ppermute | solution.py:324
  72.0 1.1 copy-start.4
  73.1 1.1 copy-start.6
  96.2 46.7 %copy-start.7 = (bf16[2,128,2560]{2,1,0:T(8,128)(2,1)S(1)}, bf16[2,128,2560]{2,1,0:T(8,128)(2,1)}, u32[]{:S(2)}) copy-start(bf16[2,128,2560]{2,1,0:T(8,128)(2,1)} %get-tuple-element.41.gl1_ref) | copy-start | bytes 3932164
  142.9 1.3 copy-start.8

commit v2 on v1

--- a/solution.py
+++ b/solution.py
@@ -28,8 +28,8 @@
     return [(n, 2 * BLK // n, cols) for n in FAR]
 
 
-def exchange(me, count, far_src, far_dst, edge_src, edge_dst, sems, prepare):
-    send_far, recv_far, send_edge, recv_edge = sems
+def exchange(me, count, edge_src, edge_dst, sems, run_far):
+    send_edge, recv_edge = sems
     barrier = pltpu.get_barrier_semaphore()
     peers = []
     for k, n in enumerate(FAR):
@@ -65,16 +65,7 @@
         def _():
             for part in range(2):
                 edge_copy(side, part).start()
-    prepare()
-    copies = []
-    for k, n, r, dest, t, o in reversed(peers):
-        copies.append(pltpu.make_async_remote_copy(
-            src_ref=far_src(k, t), dst_ref=far_dst(k, o),
-            send_sem=send_far.at[n - 1 + r], recv_sem=recv_far.at[n - 1 + r],
-            device_id={"seq": dest}, device_id_type=MESH))
-        copies[-1].start()
-    for copy in copies:
-        copy.wait()
+    run_far(peers)
     for side in range(2):
         @pl.when(has[side])
         def _():
@@ -83,9 +74,19 @@
                 edge_wait(side, part).wait_recv()
 
 
+def remote(src, dst, sems, index, device):
+    return pltpu.make_async_remote_copy(
+        src_ref=src, dst_ref=dst, send_sem=sems[0].at[index], recv_sem=sems[1].at[index],
+        device_id={"seq": device}, device_id_type=MESH)
+
+
+def columns_of(core, half):
+    return pl.ds(pl.multiple_of(core * half, HEAD_WIDTH), half)
+
+
 def sem_shapes():
     total = sum(FAR)
-    return [pltpu.SemaphoreType.DMA((total,)), pltpu.SemaphoreType.DMA((total,)),
+    return [pltpu.SemaphoreType.DMA((total,))] * 4 + [
             pltpu.SemaphoreType.DMA((2, 2)), pltpu.SemaphoreType.DMA((2, 2))]
 
 
@@ -124,16 +125,86 @@
         ref = (k_ref, v_ref)[part]
         return ref.at[pl.ds(0, BLK)] if side == 0 else ref.at[pl.ds(rows - BLK, BLK)]
 
-    exchange(me, count, lambda k, t: far_scr[k], lambda k, o: far_out[k].at[o],
-             edge_src, lambda side, part: edge_ref.at[side, part], sems, prepare)
-
-
-def send_kernel(count, g2, g3, g4, g5, eg, r2, r3, r4, r5, er, *sems):
+    half = cols // 2
+    core = me % 2
+    mine = columns_of(core, half)
+
+    def run_far(peers):
+        prepare()
+        order = peers[::-1]
+        copies = []
+        for k, n, r, dest, t, o in order:
+            src, dst = far_scr[k], far_out[k].at[o]
+            if n > 1:
+                part = columns_of(t % 2, half)
+                src, dst = src.at[:, part], dst.at[:, part]
+            copies.append(remote(src, dst, sems[:2], n - 1 + r, dest))
+            copies[-1].start()
+        swaps = []
+        for copy, (k, n, r, dest, t, o) in zip(copies, order):
+            if n > 1:
+                slot = far_out[k].at[(o + n - r) % n, :, mine]
+                pltpu.make_async_remote_copy(
+                    src_ref=slot, dst_ref=slot, send_sem=sems[0].at[n - 1 + r],
+                    recv_sem=sems[1].at[n - 1 + r],
+                    device_id={"seq": dest}, device_id_type=MESH).wait_recv()
+                swaps.append(remote(slot, slot, sems[2:4], n - 1 + r, me + 1 - 2 * core))
+                swaps[-1].start()
+                copy.wait_send()
+            else:
+                copy.wait()
+        for k, n, r, dest, t, o in order:
+            if n > 1:
+                theirs = (me + 1 - 2 * core) % n
+                slot = far_out[k].at[(theirs + n - r) % n, :, columns_of(1 - core, half)]
+                remote(slot, slot, sems[2:4], n - 1 + r, me + 1 - 2 * core).wait_recv()
+        for swap in swaps:
+            swap.wait_send()
+
+    exchange(me, count, edge_src, lambda side, part: edge_ref.at[side, part], sems[4:], run_far)
+
+
+def send_kernel(count, g2, g3, g4, g5, eg, r2, r3, r4, r5, er,
+                a3, a4, a5, b3, b4, b5, load_sem, *sems):
     me = lax.axis_index("seq")
     src, dst = (g2, g3, g4, g5), (r2, r3, r4, r5)
-    exchange(me, count, lambda k, t: src[k].at[t], lambda k, o: dst[k].at[o],
-             lambda side, part: eg.at[side, part], lambda side, part: er.at[side, part],
-             sems, lambda: None)
+    own, came = (None, a3, a4, a5), (None, b3, b4, b5)
+    half = g2.shape[-1] // 2
+    core = me % 2
+    mate = me + 1 - 2 * core
+    mine = columns_of(core, half)
+
+    def run_far(peers):
+        loads, swaps, copies = {}, {}, []
+        for k in (3, 2, 1):
+            swaps[k] = remote(src[k].at[:, :, columns_of(1 - core, half)], came[k],
+                              sems[2:4], k, mate)
+            swaps[k].start()
+            loads[k] = pltpu.make_async_copy(src[k].at[:, :, mine], own[k], load_sem.at[k])
+            loads[k].start()
+        for level in (3, 2, 1, 0):
+            if level:
+                loads[level].wait()
+                swaps[level].wait()
+
+                def add(i, _, a=own[level], b=came[level]):
+                    a[i] = (a[i].astype(F32) + b[i].astype(F32)).astype(BF16)
+                    return 0
+                lax.fori_loop(0, FAR[level], add, 0)
+            for k, n, r, dest, t, o in peers:
+                if k == level:
+                    if k:
+                        copy = remote(own[k].at[t], dst[k].at[o // 2, :, mine],
+                                      sems[:2], n - 1 + r, dest)
+                    else:
+                        copy = remote(src[k].at[t], dst[k].at[o], sems[:2], n - 1 + r, dest)
+                    copies.append(copy)
+                    copy.start()
+        for copy in copies:
+            copy.wait()
+
+    exchange(me, count, lambda side, part: eg.at[side, part],
+             lambda side, part: er.at[side, part], sems[4:], run_far)
 
 
 def keep(x, flag):
@@ -232,13 +303,15 @@
     me = lax.axis_index("seq")
     row_count, span = gk_ref.shape
     flags = (me > 0, me < count - 1)
-    row = lax.broadcasted_iota(jnp.int32, (row_count, 2 * BLK + 4 * BLK), 0)
-    col = lax.broadcasted_iota(jnp.int32, (row_count, 2 * BLK + 4 * BLK), 1)
+    sizes = [ref.shape[0] * ref.shape[1] // 2 for ref in (r2, r3, r4, r5)]
+    width = 2 * BLK + sum(sizes)
+    row = lax.broadcasted_iota(jnp.int32, (row_count, width), 0)
+    col = lax.broadcasted_iota(jnp.int32, (row_count, width), 1)
     mat = jnp.where((col < 2 * BLK) & (row // 2 == col), 0.5, 0.0)
     for k, n in enumerate(FAR):
-        first = (2 + k) * BLK
+        first = 2 * BLK + sum(sizes[:k])
         m = BLK // n
-        inside = (col >= first) & (col < first + BLK)
+        inside = (col >= first) & (col < first + sizes[k])
         mat += jnp.where(inside & (row // (4 * n) == (col - first) % m), 0.25 / n, 0.0)
     mat = mat.astype(BF16)
     for part, out in enumerate((gk_ref, gv_ref)):
@@ -246,10 +319,10 @@
         for n, ref in zip(FAR, (r2, r3, r4, r5)):
             m = BLK // n
             if m >= 16:
-                far.append(ref[:, part * m:(part + 1) * m, :].reshape(BLK, span))
+                far.append(ref[:, part * m:(part + 1) * m, :].reshape(-1, span))
             else:
                 wide = ref[...].astype(F32)
-                far.append(wide[:, part * m:(part + 1) * m].reshape(BLK, span).astype(BF16))
+                far.append(wide[:, part * m:(part + 1) * m].reshape(-1, span).astype(BF16))
         total = loc_ref[part] + dot(mat, jnp.concatenate(far, 0), NN)
         low = jnp.where(flags[0], er_ref[0, part].astype(F32), 0.0)
         high = jnp.where(flags[1], er_ref[1, part].astype(F32), 0.0)
@@ -339,12 +412,14 @@
         name="differentiate",
     )(*common, att, lse, coef)
 
+    summed = [(max(1, s[0] // 2),) + s[1:] for s in pieces]
+    halves = [pltpu.VMEM(s[:2] + (cols // 2,), BF16) for s in pieces[1:]]
     back = pl.pallas_call(
         functools.partial(send_kernel, count),
-        out_shape=piece_out + [edge_out],
+        out_shape=[shape(s, BF16) for s in summed] + [edge_out],
         in_specs=[any_spec] * 5,
         out_specs=[any_spec] * 5,
-        scratch_shapes=sem_shapes(),
+        scratch_shapes=halves * 2 + [pltpu.SemaphoreType.DMA((LEV - 1,))] + sem_shapes(),
         compiler_params=pltpu.CompilerParams(
             collective_id=1, has_side_effects=True, vmem_limit_bytes=limit),
         name="send_terms",
@@ -354,7 +429,8 @@
         functools.partial(combine_kernel, count),
         grid=grid,
         out_shape=[shape((rows, cols), BF16)] * 2,
-        in_specs=[cube(2, rows), cube(2, rows // 2)] + piece_specs + [quad],
+        in_specs=[cube(2, rows), cube(2, rows // 2)]
+        + [cube(s[0], s[1]) for s in summed] + [quad],
         out_specs=[flat(rows)] * 2,
         compiler_params=params,
         name="combine",

time: 152 us -> 125 us (0.82)
  Pallas kernels: 138 us -> 114 us
    pallas_call x1, Pallas kernels: 46.7 us -> 33.4 us  [body(): pl.pallas_call(functools.partial(send_kernel, count), out_shape=[shape(s,...]
    pallas_call x1, Pallas kernels: 48.7 us -> 37.7 us  [body(): pl.pallas_call(functools.partial(gather_kernel, count), out_shape=[shape(...]
    unnamed x20 -> x18, local copies, waits for them, and re-layouts: 6.75 us -> 5.39 us
where the time goes in v2:
time: 125 us
  Pallas kernels  114 us (91%)
  local copies, waits for them, and re-layouts  6.38 us (5%)
  waiting for transfers between devices  2.21 us (2%)
    pallas_call x1, Pallas kernels, body(): pl.pallas_call(functools.partial(gather_kernel, count), out_shape=[shape(...  37.7 us
    pallas_call x1, Pallas kernels, body(): pl.pallas_call(functools.partial(send_kernel, count), out_shape=[shape(s,...  33.4 us
    pallas_call x1, Pallas kernels, body(): pl.pallas_call(functools.partial(backward_kernel, count), grid=grid, out_...  22 us
    pallas_call x1, Pallas kernels, body(): pl.pallas_call(functools.partial(forward_kernel, count), grid=grid, out_s...  15.1 us
    pallas_call x1, Pallas kernels, body(): pl.pallas_call(functools.partial(combine_kernel, count), grid=grid, out_s...  6.03 us
    unnamed x18, local copies, waits for them, and re-layouts  5.39 us
  transfers between devices with their start and end apart: 1, of which 1 were waited for; matrix products, arithmetic and copies ran while one was open for 0% of the time, Pallas kernels for 0%

profile of v2, /device:TPU:13, one launch (start us, length us, event | category | flops | bytes accessed | tf_op | source)
XLA Modules:
  0.0 124.6 jit_solution(8941866913939360643)
XLA Ops:
  0.7 0.1 broadcast_in_dim.23
  0.8 0.1 reshape.247
  0.8 0.7 reshape.246.gain_ref
  1.5 0.1 fusion.1
  1.6 0.1 compare_and_fusion
  1.7 0.2 and_select_fusion
  1.9 0.1 pad_maximum_fusion.bias_ref
  2.1 0.0 copy-start
  2.1 37.7 %gather_tiles.1 = (bf16[2,128,2560]{2,1,0:T(8,128)(2,1)S(1)}, bf16[1,128,2560]{2,1,0:T(8,128)(2,1)S(1)}, bf16[2,64,2560]{2,1,0:T(8,128)(2,1)S(1)}, bf16[4,32,256...) custom-call(bf16[256,2560]{1,0:T(8,128)(2,1)} %k_ref.5, ...), custom_call_target="tpu_custom_call" | custom-call | tf_op jit(solution)/shard_map/gather_tiles/pallas_call | solution.py:358
  39.8 0.0 copy-start.1
  39.9 1.0 copy-done.1
  40.9 0.0 copy-start.2
  40.9 1.1 copy-done.2
  42.0 0.0 copy-start.3
  42.0 0.0 copy-start.5
  42.0 0.0 copy-done
  42.0 15.1 %attend.1 = (bf16[256,2560]{1,0:T(8,128)(2,1)S(1)}, f32[20,1,256]{2,1,0:T(1,128)S(1)}, f32[2,256,128]{2,1,0:T(8,128)S(1)}) custom-call(bf16[256,2560]{1,0:T(8,128)(2,1)S(1)} %copy-done, bf16[256,2560]{1,0:T(8,128)(2,1)} %k_ref.5, bf16[256,2560]{1,0:T(8,128)(2,1)} %v_ref.5, bf16[256,2560]{1,0:T(8,128)(2,1)} %u_ref.3, bf16[1,2560]{1,0:T(2,128)(2,1)S(1)} %reshape.246.gain_ref, ...), custom_call_target="tpu_custom_call" | custom-call | tf_op jit(solution)/shard_map/attend/pallas_call | solution.py:382
  57.0 0.0 copy-done.3
  57.0 0.0 copy-done.5
  57.1 0.0 copy-start.8
  57.1 1.1 copy-done.8
  58.2 0.1 reduce_sum.9
  58.3 0.3 collective-permute-start
  58.6 2.2 %collective-permute-done = f32[2,256]{1,0:T(2,128)S(1)} collective-permute-done((f32[2,256]{1,0:T(2,128)S(1)}, f32[2,256]{1,0:T(2,128)S(1)}, u32[]{:S(2)}, u32[]{:S(2)}) %collective-permute-start) | collective-permute-done | bytes 2080 | tf_op jit(solution)/shard_map/ppermute | solution.py:397
  60.8 0.1 copy.14.coef_ref
  61.0 0.0 copy-start.4
  61.0 1.1 copy-done.4
  62.1 1.1 copy-done.6
  63.2 22.0 %differentiate.1 = (bf16[256,2560]{1,0:T(8,128)(2,1)}, bf16[256,2560]{1,0:T(8,128)(2,1)}, f32[2,256,2560]{2,1,0:T(8,128)}, bf16[2,128,2560]{2,1,0:T(8,128)(2,1)}...) custom-call(bf16[256,2560]{1,0:T(8,128)(2,1)} %q_ref.3, ...), custom_call_target="tpu_custom_call" | custom-call | tf_op jit(solution)/shard_map/differentiate/pallas_call | solution.py:403
  85.2 33.4 %send_terms.1 = (bf16[1,128,2560]{2,1,0:T(8,128)(2,1)S(1)}, bf16[1,64,2560]{2,1,0:T(8,128)(2,1)S(1)}, bf16[2,32,2560]{2,1,0:T(8,128)(2,1)S(1)}, bf16[4,16,2560]{...) custom-call(bf16[1,128,2560]{2,1,0:T(8,128)(2,1)S(1)} %get-tuple-element.42.g2, ...), custom_call_target="tpu_custom_call" | custom-call | tf_op jit(solution)/shard_map/send_terms/pallas_call | solution.py:417
  118.6 0.0 copy-done.7
  118.6 6.0 %combine.1 = (bf16[256,2560]{1,0:T(8,128)(2,1)}, bf16[256,2560]{1,0:T(8,128)(2,1)}) custom-call(f32[2,256,2560]{2,1,0:T(8,128)} %get-tuple-element.40.loc_ref, bf16[2,128,2560]{2,1,0:T(8,128)(2,1)S(1)} %copy-done.7, bf16[1,128,2560]{2,1,0:T(8,128)(2,1)S(1)} %get-tuple-element.47.r2, bf16[1,64,2560]{2,1,0:T(8,128)(2,1)S(1)} %get-tuple-element.48.r3, ...), custom_call_target="tpu_custom_call" | custom-call | tf_op jit(solution)/shard_map/combine/pallas_call | solution.py:428
  (10 shorter events, 0.1 us)
Async XLA Ops:
  2.1 39.9 %copy-start = (bf16[256,2560]{1,0:T(8,128)(2,1)S(1)}, bf16[256,2560]{1,0:T(8,128)(2,1)}, u32[]{:S(2)}) copy-start(bf16[256,2560]{1,0:T(8,128)(2,1)} %q_ref.3) | copy-start | bytes 3932164
  39.8 1.1 copy-start.1
  40.9 1.1 copy-start.2
  42.0 15.1 %copy-start.3 = (bf16[4,32,2560]{2,1,0:T(8,128)(2,1)}, bf16[4,32,2560]{2,1,0:T(8,128)(2,1)S(1)}, u32[]{:S(2)}) copy-start(bf16[4,32,2560]{2,1,0:T(8,128)(2,1)S(1)} %get-tuple-element.32.r4) | copy-start | bytes 1966084
  42.0 15.1 %copy-start.5 = (bf16[8,16,2560]{2,1,0:T(8,128)(2,1)}, bf16[8,16,2560]{2,1,0:T(8,128)(2,1)S(1)}, u32[]{:S(2)}) copy-start(bf16[8,16,2560]{2,1,0:T(8,128)(2,1)S(1)} %get-tuple-element.33.r5) | copy-start | bytes 1966084
  57.1 1.1 copy-start.8
  58.3 2.5 %collective-permute-start = (f32[2,256]{1,0:T(2,128)S(1)}, f32[2,256]{1,0:T(2,128)S(1)}, u32[]{:S(2)}, u32[]{:S(2)}) collective-permute-start(f32[2,256]{1,0:T(2,128)S(1)} %reduce_sum.9), channel_id=1, source_target_pairs={{0,1},{1,0},{2,3},{3,2},{4,5},{5,4},{6,7},{7,6},{8,9},{9,8},{10,11... | collective-permute-start | bytes 6152 | tf_op jit(solution)/shard_map/ppermute | solution.py:397
  61.0 1.1 copy-start.4
  62.1 1.1 copy-start.6
  85.2 33.4 %copy-start.7 = (bf16[2,128,2560]{2,1,0:T(8,128)(2,1)S(1)}, bf16[2,128,2560]{2,1,0:T(8,128)(2,1)}, u32[]{:S(2)}) copy-start(bf16[2,128,2560]{2,1,0:T(8,128)(2,1)} %get-tuple-element.41.gl1_ref) | copy-start | bytes 3932164

commit v3 on v2

--- a/solution.py
+++ b/solution.py
@@ -28,17 +28,18 @@
     return [(n, 2 * BLK // n, cols) for n in FAR]
 
 
-def exchange(me, count, edge_src, edge_dst, sems, run_far):
-    send_edge, recv_edge = sems
-    barrier = pltpu.get_barrier_semaphore()
+def relations(me, count):
     peers = []
     for k, n in enumerate(FAR):
         g, o = me // n, me % n
         base = (g + 1 - 2 * (g % 2)) * n
         for r in range(n):
             peers.append((k, n, r, base + (o + r) % n, (o + r) % n, o))
-    has = (me > 0, me < count - 1)
-    ids = (me - 1, me + 1)
+    return peers, (me > 0, me < count - 1), (me - 1, me + 1)
+
+
+def greet(peers, has, ids):
+    barrier = pltpu.get_barrier_semaphore()
     for peer in peers:
         pl.semaphore_signal(barrier, inc=1, device_id={"seq": peer[3]}, device_id_type=MESH)
     for side in range(2):
@@ -47,6 +48,12 @@
             pl.semaphore_signal(barrier, inc=1, device_id={"seq": ids[side]}, device_id_type=MESH)
     pl.semaphore_wait(
         barrier, len(peers) + has[0].astype(jnp.int32) + has[1].astype(jnp.int32))
+
+
+def exchange(me, count, edge_src, edge_dst, sems, run_far):
+    send_edge, recv_edge = sems
+    peers, has, ids = relations(me, count)
+    greet(peers, has, ids)
 
     def edge_copy(side, part):
         return pltpu.make_async_remote_copy(
@@ -76,7 +83,9 @@
 
 def remote(src, dst, sems, index, device):
     return pltpu.make_async_remote_copy(
-        src_ref=src, dst_ref=dst, send_sem=sems[0].at[index], recv_sem=sems[1].at[index],
+        src_ref=src, dst_ref=dst,
+        send_sem=sems[0] if index is None else sems[0].at[index],
+        recv_sem=sems[1] if index is None else sems[1].at[index],
         device_id={"seq": device}, device_id_type=MESH)
 
 
@@ -162,49 +171,6 @@
             swap.wait_send()
 
     exchange(me, count, edge_src, lambda side, part: edge_ref.at[side, part], sems[4:], run_far)
-
-
-def send_kernel(count, g2, g3, g4, g5, eg, r2, r3, r4, r5, er,
-                a3, a4, a5, b3, b4, b5, load_sem, *sems):
-    me = lax.axis_index("seq")
-    src, dst = (g2, g3, g4, g5), (r2, r3, r4, r5)
-    own, came = (None, a3, a4, a5), (None, b3, b4, b5)
-    half = g2.shape[-1] // 2
-    core = me % 2
-    mate = me + 1 - 2 * core
-    mine = columns_of(core, half)
-
-    def run_far(peers):
-        loads, swaps, copies = {}, {}, []
-        for k in (3, 2, 1):
-            swaps[k] = remote(src[k].at[:, :, columns_of(1 - core, half)], came[k],
-                              sems[2:4], k, mate)
-            swaps[k].start()
-            loads[k] = pltpu.make_async_copy(src[k].at[:, :, mine], own[k], load_sem.at[k])
-            loads[k].start()
-        for level in (3, 2, 1, 0):
-            if level:
-                loads[level].wait()
-                swaps[level].wait()
-
-                def add(i, _, a=own[level], b=came[level]):
-                    a[i] = (a[i].astype(F32) + b[i].astype(F32)).astype(BF16)
-                    return 0
-                lax.fori_loop(0, FAR[level], add, 0)
-            for k, n, r, dest, t, o in peers:
-                if k == level:
-                    if k:
-                        copy = remote(own[k].at[t], dst[k].at[o // 2, :, mine],
-                                      sems[:2], n - 1 + r, dest)
-                    else:
-                        copy = remote(src[k].at[t], dst[k].at[o], sems[:2], n - 1 + r, dest)
-                    copies.append(copy)
-                    copy.start()
-        for copy in copies:
-            copy.wait()
-
-    exchange(me, count, lambda side, part: eg.at[side, part],
-             lambda side, part: er.at[side, part], sems[4:], run_far)
 
 
 def keep(x, flag):
@@ -299,6 +265,81 @@
             g[:, :, c] = jnp.concatenate(parts, 1).astype(BF16)
 
 
+def derive_send_kernel(count, steps, *refs):
+    ins, outs = refs[:15], refs[15:19]
+    dst, er = refs[19:23], refs[23]
+    g, eg, own, came = refs[24:28], refs[28], (None,) + refs[29:32], (None,) + refs[32:35]
+    far_sems, swap_sems, edge_sems = refs[35:37], refs[37:39], refs[39:41]
+    me = lax.axis_index("seq")
+    i = pl.program_id(0)
+    step = HEADS_STEP * HEAD_WIDTH
+    half = step // 2
+    core = me % 2
+    mate = me + 1 - 2 * core
+    peers, has, ids = relations(me, count)
+
+    @pl.when(i == 0)
+    def _():
+        greet(peers, has, ids)
+
+    backward_kernel(count, *ins, *outs, *[ref.at[i] for ref in g], eg.at[i])
+
+    def chunk(j):
+        return pl.ds(pl.multiple_of(j * step, HEAD_WIDTH), step)
+
+    def edge(j, side, slot):
+        return remote(eg.at[j, side], er.at[slot, :, :, chunk(j)],
+                      (edge_sems[0].at[j, side], edge_sems[1].at[j, slot]), None, ids[side])
+
+    def swap(j, k):
+        return remote(g[k].at[j, :, :, columns_of(1 - core, half)], came[k].at[j],
+                      (swap_sems[0].at[j, k], swap_sems[1].at[j, k]), None, mate)
+
+    def far(j, peer):
+        k, n, r, dest, t, o = peer
+        sems = (far_sems[0].at[j, n - 1 + r], far_sems[1].at[j, n - 1 + r])
+        if k == 0:
+            return remote(g[0].at[j, t], dst[0].at[o, :, chunk(j)], sems, None, dest)
+        place = pl.ds(pl.multiple_of(j * step + core * half, HEAD_WIDTH), half)
+        return remote(own[k].at[j, t], dst[k].at[o // 2, :, place], sems, None, dest)
+
+    for k in (3, 2, 1):
+        swap(i, k).start()
+    for side in range(2):
+        @pl.when(has[side])
+        def _():
+            edge(i, side, 1 - side).start()
+    far(i, peers[0]).start()
+
+    def send_sums(j):
+        for level in (3, 2, 1):
+            swap(j, level).wait()
+            mine = g[level][j, :, :, columns_of(core, half)].astype(F32)
+            own[level][j] = (mine + came[level][j].astype(F32)).astype(BF16)
+            for peer in peers:
+                if peer[0] == level:
+                    far(j, peer).start()
+
+    @pl.when(i > 0)
+    def _():
+        send_sums(i - 1)
+
+    @pl.when(i == steps - 1)
+    def _():
+        send_sums(i)
+
+        def finish(j, _):
+            for peer in peers:
+                far(j, peer).wait()
+            for side in range(2):
+                @pl.when(has[side])
+                def _():
+                    edge(j, side, 1 - side).wait_send()
+                    edge(j, side, side).wait_recv()
+            return 0
+        lax.fori_loop(0, steps, finish, 0)
+
+
 def combine_kernel(count, loc_ref, gl1_ref, r2, r3, r4, r5, er_ref, gk_ref, gv_ref):
     me = lax.axis_index("seq")
     row_count, span = gk_ref.shape
@@ -400,30 +441,25 @@
     inv = lax.rsqrt(total[0] / columns + EPSILON)
     coef = jnp.stack([inv, inv * inv * inv * total[1] / columns], 1)
 
-    normed, gq, loc, gl1, *grads = pl.pallas_call(
-        functools.partial(backward_kernel, count),
+    steps = grid[0]
+    summed = [(max(1, s[0] // 2),) + s[1:] for s in pieces]
+    chunks = [pltpu.VMEM((steps,) + s[:2] + (step,), BF16) for s in pieces]
+    halves = [pltpu.VMEM((steps,) + s[:2] + (step // 2,), BF16) for s in pieces[1:]]
+    dma = pltpu.SemaphoreType.DMA
+    normed, gq, loc, gl1, *back = pl.pallas_call(
+        functools.partial(derive_send_kernel, count, steps),
         grid=grid,
         out_shape=[shape((rows, cols), BF16)] * 2
         + [shape((2, rows, cols), F32), shape((2, rows // 2, cols), BF16)]
-        + piece_out + [edge_out],
+        + [shape(s, BF16) for s in summed] + [edge_out],
         in_specs=shared + [flat(rows), lse_spec, fixed((rows, 2))],
-        out_specs=[flat(rows)] * 2 + [cube(2, rows), cube(2, rows // 2)] + piece_specs + [quad],
-        compiler_params=params,
-        name="differentiate",
-    )(*common, att, lse, coef)
-
-    summed = [(max(1, s[0] // 2),) + s[1:] for s in pieces]
-    halves = [pltpu.VMEM(s[:2] + (cols // 2,), BF16) for s in pieces[1:]]
-    back = pl.pallas_call(
-        functools.partial(send_kernel, count),
-        out_shape=[shape(s, BF16) for s in summed] + [edge_out],
-        in_specs=[any_spec] * 5,
-        out_specs=[any_spec] * 5,
-        scratch_shapes=halves * 2 + [pltpu.SemaphoreType.DMA((LEV - 1,))] + sem_shapes(),
+        out_specs=[flat(rows)] * 2 + [cube(2, rows), cube(2, rows // 2)] + [any_spec] * 5,
+        scratch_shapes=chunks + [pltpu.VMEM((steps, 2, 2, BLK, step), BF16)] + halves * 2
+        + [dma((steps, sum(FAR)))] * 2 + [dma((steps, LEV - 1))] * 2 + [dma((steps, 2))] * 2,
         compiler_params=pltpu.CompilerParams(
             collective_id=1, has_side_effects=True, vmem_limit_bytes=limit),
-        name="send_terms",
-    )(*grads)
+        name="differentiate_and_send",
+    )(*common, att, lse, coef)
 
     gk, gv = pl.pallas_call(
         functools.partial(combine_kernel, count),

time: 125 us -> 117 us (0.936)
  Pallas kernels: 114 us -> 101 us
  local copies, waits for them, and re-layouts: 6.38 us -> 11.8 us
    pallas_call x2 -> x1, Pallas kernels: 55.4 us -> 41.7 us  [body(): pl.pallas_call(functools.partial(derive_send_kernel, count, steps), grid=...]
    unnamed x18 -> x26, local copies, waits for them, and re-layouts: 5.39 us -> 10.8 us
where the time goes in v3:
time: 117 us; the launch traced here: 116 us
  Pallas kernels  101 us (86%)
  local copies, waits for them, and re-layouts  11.8 us (10%)
  waiting for transfers between devices  2.21 us (2%)
    pallas_call x1, Pallas kernels, body(): pl.pallas_call(functools.partial(derive_send_kernel, count, steps), grid=...  41.7 us
    pallas_call x1, Pallas kernels, body(): pl.pallas_call(functools.partial(gather_kernel, count), out_shape=[shape(...  37.7 us
    pallas_call x1, Pallas kernels, body(): pl.pallas_call(functools.partial(forward_kernel, count), grid=grid, out_s...  15.1 us
    unnamed x26, local copies, waits for them, and re-layouts  10.8 us
    pallas_call x1, Pallas kernels, body(): pl.pallas_call(functools.partial(combine_kernel, count), grid=grid, out_s...  6.13 us
  transfers between devices with their start and end apart: 1, of which 1 were waited for; matrix products, arithmetic and copies ran while one was open for 0% of the time, Pallas kernels for 0%

profile of v3, /device:TPU:13, one launch (start us, length us, event | category | flops | bytes accessed | tf_op | source)
XLA Modules:
  0.0 116.4 jit_solution(9585503566211293807)
XLA Ops:
  0.7 0.1 broadcast_in_dim.23
  0.8 0.1 reshape.247
  0.8 0.7 reshape.246.gain_ref.refs_4_
  1.5 0.1 fusion.1
  1.6 0.1 compare_and_fusion
  1.7 0.2 and_select_fusion
  1.9 0.1 pad_maximum_fusion.bias_ref.refs_5_
  2.1 0.0 copy-start
  2.1 37.7 %gather_tiles.1 = (bf16[2,128,2560]{2,1,0:T(8,128)(2,1)S(1)}, bf16[1,128,2560]{2,1,0:T(8,128)(2,1)S(1)}, bf16[2,64,2560]{2,1,0:T(8,128)(2,1)S(1)}, bf16[4,32,256...) custom-call(bf16[256,2560]{1,0:T(8,128)(2,1)} %refs_1_.1, ...), custom_call_target="tpu_custom_call" | custom-call | tf_op jit(solution)/shard_map/gather_tiles/pallas_call | solution.py:399
  39.8 0.0 copy-start.1
  39.9 1.0 copy-done.1
  40.9 1.1 copy-done.2
  42.0 0.0 copy-done
  42.0 15.1 %attend.1 = (bf16[256,2560]{1,0:T(8,128)(2,1)S(1)}, f32[20,1,256]{2,1,0:T(1,128)S(1)}, f32[2,256,128]{2,1,0:T(8,128)S(1)}) custom-call(bf16[256,2560]{1,0:T(8,128)(2,1)S(1)} %copy-done, bf16[256,2560]{1,0:T(8,128)(2,1)} %refs_1_.1, bf16[256,2560]{1,0:T(8,128)(2,1)} %refs_2_.1, bf16[256,2560]{1,0:T(8,128)(2,1)} %refs_3_.1, ...), custom_call_target="tpu_custom_call" | custom-call | tf_op jit(solution)/shard_map/attend/pallas_call | solution.py:423
  57.0 0.0 copy-done.3
  57.1 0.0 copy-start.9
  57.1 1.0 copy-done.9
  58.1 0.1 reduce_sum.9
  58.3 0.3 collective-permute-start
  58.6 2.2 %collective-permute-done = f32[2,256]{1,0:T(2,128)S(1)} collective-permute-done((f32[2,256]{1,0:T(2,128)S(1)}, f32[2,256]{1,0:T(2,128)S(1)}, u32[]{:S(2)}, u32[]{:S(2)}) %collective-permute-start) | collective-permute-done | bytes 2080 | tf_op jit(solution)/shard_map/ppermute | solution.py:438
  60.8 0.1 copy.14.refs_14_
  60.9 0.0 copy-start.4
  61.0 1.1 copy-done.4
  62.0 1.1 copy-done.6
  63.1 41.7 %differentiate_and_send.1 = (bf16[256,2560]{1,0:T(8,128)(2,1)}, bf16[256,2560]{1,0:T(8,128)(2,1)}, f32[2,256,2560]{2,1,0:T(8,128)}, bf16[2,128,2560]{2,1,0:T(8,1...) custom-call(bf16[256,2560]{1,0:T(8,128)(2,1)} %refs_0_.1, ...), custom_call_target="tpu_custom_call" | custom-call | tf_op jit(solution)/shard_map/differentiate_and_send/pallas_call | solution.py:449
  104.8 1.3 %copy-done.7 = bf16[2,128,2560]{2,1,0:T(8,128)(2,1)S(1)} copy-done((bf16[2,128,2560]{2,1,0:T(8,128)(2,1)S(1)}, bf16[2,128,2560]{2,1,0:T(8,128)(2,1)}, u32[]{:S(2)}) %copy-start.7) | copy-done | bytes 1310744
  106.1 1.3 %copy-done.8 = bf16[2,2,64,2560]{3,2,1,0:T(8,128)(2,1)S(1)} copy-done((bf16[2,2,64,2560]{3,2,1,0:T(8,128)(2,1)S(1)}, bf16[2,2,64,2560]{3,2,1,0:T(8,128)(2,1)}, u32[]{:S(2)}) %copy-start.8) | copy-done | bytes 1310744
  107.4 6.1 %combine.1 = (bf16[256,2560]{1,0:T(8,128)(2,1)}, bf16[256,2560]{1,0:T(8,128)(2,1)}) custom-call(f32[2,256,2560]{2,1,0:T(8,128)} %get-tuple-element.35.loc_ref, bf16[2,128,2560]{2,1,0:T(8,128)(2,1)S(1)} %copy-done.7, bf16[1,128,2560]{2,1,0:T(8,128)(2,1)S(1)} %get-tuple-element.37.r2, bf16[1,64,2560]{2,1,0:T(8,128)(2,1)S(1)} %get-tuple-element.38.r3, ...), custom_call_target="tpu_custom_call" | custom-call | tf_op jit(solution)/shard_map/combine/pallas_call | solution.py:464
  113.6 0.0 copy-done.11
  113.6 1.1 copy.17
  114.6 0.7 copy-done.10
  115.4 1.1 copy.18
  (17 shorter events, 0.1 us)
Async XLA Ops:
  2.1 39.9 %copy-start = (bf16[256,2560]{1,0:T(8,128)(2,1)S(1)}, bf16[256,2560]{1,0:T(8,128)(2,1)}, u32[]{:S(2)}) copy-start(bf16[256,2560]{1,0:T(8,128)(2,1)} %refs_0_.1) | copy-start | bytes 3932164
  39.8 1.1 copy-start.1
  40.9 1.1 copy-start.2
  42.0 15.1 %copy-start.3 = (bf16[4,32,2560]{2,1,0:T(8,128)(2,1)}, bf16[4,32,2560]{2,1,0:T(8,128)(2,1)S(1)}, u32[]{:S(2)}) copy-start(bf16[4,32,2560]{2,1,0:T(8,128)(2,1)S(1)} %get-tuple-element.27.r4.refs_9_) | copy-start | bytes 1966084
  42.0 15.1 %copy-start.5 = (bf16[8,16,2560]{2,1,0:T(8,128)(2,1)}, bf16[8,16,2560]{2,1,0:T(8,128)(2,1)S(1)}, u32[]{:S(2)}) copy-start(bf16[8,16,2560]{2,1,0:T(8,128)(2,1)S(1)} %get-tuple-element.28.r5.refs_10_) | copy-start | bytes 1966084
  57.1 1.1 copy-start.9
  58.3 2.5 %collective-permute-start = (f32[2,256]{1,0:T(2,128)S(1)}, f32[2,256]{1,0:T(2,128)S(1)}, u32[]{:S(2)}, u32[]{:S(2)}) collective-permute-start(f32[2,256]{1,0:T(2,128)S(1)} %reduce_sum.9), channel_id=1, source_target_pairs={{0,1},{1,0},{2,3},{3,2},{4,5},{5,4},{6,7},{7,6},{8,9},{9,8},{10,11... | collective-permute-start | bytes 6152 | tf_op jit(solution)/shard_map/ppermute | solution.py:438
  60.9 1.1 copy-start.4
  62.0 1.1 copy-start.6
  104.8 1.3 %copy-start.7 = (bf16[2,128,2560]{2,1,0:T(8,128)(2,1)S(1)}, bf16[2,128,2560]{2,1,0:T(8,128)(2,1)}, u32[]{:S(2)}) copy-start(bf16[2,128,2560]{2,1,0:T(8,128)(2,1)} %get-tuple-element.36.gl1_ref) | copy-start | bytes 3932164
  106.1 1.3 %copy-start.8 = (bf16[2,2,64,2560]{3,2,1,0:T(8,128)(2,1)S(1)}, bf16[2,2,64,2560]{3,2,1,0:T(8,128)(2,1)}, u32[]{:S(2)}) copy-start(bf16[2,2,64,2560]{3,2,1,0:T(8,128)(2,1)} %get-tuple-element.41.er_ref) | copy-start | bytes 3932164
  107.4 6.1 %copy-start.11 = (bf16[256,2560]{1,0:T(8,128)(2,1)S(1)}, bf16[256,2560]{1,0:T(8,128)(2,1)}, u32[]{:S(2)}) copy-start(bf16[256,2560]{1,0:T(8,128)(2,1)} %get-tuple-element.54) | copy-start | bytes 3932164
  113.6 1.8 %copy-start.10 = (bf16[256,2560]{1,0:T(8,128)(2,1)S(1)}, bf16[256,2560]{1,0:T(8,128)(2,1)}, u32[]{:S(2)}) copy-start(bf16[256,2560]{1,0:T(8,128)(2,1)} %get-tuple-element.55) | copy-start | bytes 3932164

commit v4 on v3

--- a/solution.py
+++ b/solution.py
@@ -50,37 +50,6 @@
         barrier, len(peers) + has[0].astype(jnp.int32) + has[1].astype(jnp.int32))
 
 
-def exchange(me, count, edge_src, edge_dst, sems, run_far):
-    send_edge, recv_edge = sems
-    peers, has, ids = relations(me, count)
-    greet(peers, has, ids)
-
-    def edge_copy(side, part):
-        return pltpu.make_async_remote_copy(
-            src_ref=edge_src(side, part), dst_ref=edge_dst(1 - side, part),
-            send_sem=send_edge.at[side, part], recv_sem=recv_edge.at[1 - side, part],
-            device_id={"seq": ids[side]}, device_id_type=MESH)
-
-    def edge_wait(side, part):
-        return pltpu.make_async_remote_copy(
-            src_ref=edge_src(side, part), dst_ref=edge_dst(side, part),
-            send_sem=send_edge.at[side, part], recv_sem=recv_edge.at[side, part],
-            device_id={"seq": ids[side]}, device_id_type=MESH)
-
-    for side in range(2):
-        @pl.when(has[side])
-        def _():
-            for part in range(2):
-                edge_copy(side, part).start()
-    run_far(peers)
-    for side in range(2):
-        @pl.when(has[side])
-        def _():
-            for part in range(2):
-                edge_wait(side, part).wait_send()
-                edge_wait(side, part).wait_recv()
-
-
 def remote(src, dst, sems, index, device):
     return pltpu.make_async_remote_copy(
         src_ref=src, dst_ref=dst,
@@ -93,84 +62,12 @@
     return pl.ds(pl.multiple_of(core * half, HEAD_WIDTH), half)
 
 
-def sem_shapes():
-    total = sum(FAR)
-    return [pltpu.SemaphoreType.DMA((total,))] * 4 + [
-            pltpu.SemaphoreType.DMA((2, 2)), pltpu.SemaphoreType.DMA((2, 2))]
-
-
 def halve(x):
     n = x.shape[0]
     row = lax.broadcasted_iota(jnp.int32, (n // 2, n), 0)
     col = lax.broadcasted_iota(jnp.int32, (n // 2, n), 1)
     mat = jnp.where((col == 2 * row) | (col == 2 * row + 1), 0.5, 0.0).astype(BF16)
     return dot(mat, x, NN)
-
-
-def gather_kernel(count, k_ref, v_ref, l1_ref, r2, r3, r4, r5, edge_ref,
-                  s2, s3, s4, s5, *sems):
-    me = lax.axis_index("seq")
-    rows, cols = k_ref.shape
-    far_scr, far_out = (s2, s3, s4, s5), (r2, r3, r4, r5)
-    width = 4 * HEAD_WIDTH
-
-    def prepare():
-        def step(i, _):
-            c = pl.ds(pl.multiple_of(i * width, width), width)
-            for part, ref in enumerate((k_ref, v_ref)):
-                level = halve(ref[:, c]).astype(BF16)
-                l1_ref[part, :, c] = level
-                for scr, n in zip((s2, s3, s4), FAR):
-                    level = halve(level).astype(BF16)
-                    m = BLK // n
-                    scr[part * m:(part + 1) * m, c] = level
-            last = jnp.concatenate(
-                [halve(s4[:16, c]), halve(s4[16:, c])], 0)
-            s5[:, c] = last.astype(BF16)
-            return 0
-        lax.fori_loop(0, cols // width, step, 0)
-
-    def edge_src(side, part):
-        ref = (k_ref, v_ref)[part]
-        return ref.at[pl.ds(0, BLK)] if side == 0 else ref.at[pl.ds(rows - BLK, BLK)]
-
-    half = cols // 2
-    core = me % 2
-    mine = columns_of(core, half)
-
-    def run_far(peers):
-        prepare()
-        order = peers[::-1]
-        copies = []
-        for k, n, r, dest, t, o in order:
-            src, dst = far_scr[k], far_out[k].at[o]
-            if n > 1:
-                part = columns_of(t % 2, half)
-                src, dst = src.at[:, part], dst.at[:, part]
-            copies.append(remote(src, dst, sems[:2], n - 1 + r, dest))
-            copies[-1].start()
-        swaps = []
-        for copy, (k, n, r, dest, t, o) in zip(copies, order):
-            if n > 1:
-                slot = far_out[k].at[(o + n - r) % n, :, mine]
-                pltpu.make_async_remote_copy(
-                    src_ref=slot, dst_ref=slot, send_sem=sems[0].at[n - 1 + r],
-                    recv_sem=sems[1].at[n - 1 + r],
-                    device_id={"seq": dest}, device_id_type=MESH).wait_recv()
-                swaps.append(remote(slot, slot, sems[2:4], n - 1 + r, me + 1 - 2 * core))
-                swaps[-1].start()
-                copy.wait_send()
-            else:
-                copy.wait()
-        for k, n, r, dest, t, o in order:
-            if n > 1:
-                theirs = (me + 1 - 2 * core) % n
-                slot = far_out[k].at[(theirs + n - r) % n, :, columns_of(1 - core, half)]
-                remote(slot, slot, sems[2:4], n - 1 + r, me + 1 - 2 * core).wait_recv()
-        for swap in swaps:
-            swap.wait_send()
-
-    exchange(me, count, edge_src, lambda side, part: edge_ref.at[side, part], sems[4:], run_far)
 
 
 def keep(x, flag):
@@ -223,6 +120,121 @@
             sg = u_ref[rows, c].astype(F32) * gain
             stat_ref[0, rows, :] += wide * wide
             stat_ref[1, rows, :] += sg * wide
+
+
+def gather_attend_kernel(count, steps, *refs):
+    q_ref, k_ref, v_ref, u_ref, gain_ref, bias_ref = refs[:6]
+    stats, outs = refs[6:9], refs[9:15]
+    l1, recv, er, coarse = refs[15], refs[16:20], refs[20], refs[21:25]
+    far_sems, swap_sems, edge_sems, out_sem = refs[25:27], refs[27:29], refs[29:31], refs[31]
+    me = lax.axis_index("seq")
+    i = pl.program_id(0)
+    rows = k_ref.shape[0]
+    step = HEADS_STEP * HEAD_WIDTH
+    half = step // 2
+    core = me % 2
+    mate = me + 1 - 2 * core
+    peers, has, ids = relations(me, count)
+    order = peers[::-1]
+
+    def chunk(j):
+        return pl.ds(pl.multiple_of(j * step, HEAD_WIDTH), step)
+
+    def edge(j, side, part, slot):
+        ref = (k_ref, v_ref)[part]
+        src = ref.at[pl.ds(side * (rows - BLK), BLK), chunk(j)]
+        return remote(src, er.at[j, slot, part],
+                      (edge_sems[0].at[j, side, part], edge_sems[1].at[j, slot, part]),
+                      None, ids[side])
+
+    def far(j, peer):
+        k, n, r, dest, t, o = peer
+        sems = (far_sems[0].at[j, n - 1 + r], far_sems[1].at[j, n - 1 + r])
+        if n == 1:
+            return remote(coarse[0].at[j], recv[0].at[j, 0], sems, None, dest)
+        part = columns_of(t % 2, half)
+        return remote(coarse[k].at[j, :, part], recv[k].at[j, o, :, part], sems, None, dest)
+
+    def swap(j, peer, owner, side, sems):
+        k, n, r = peer[:3]
+        slot = recv[k].at[j, (owner % n + n - r) % n, :, columns_of(side, half)]
+        return remote(slot, slot,
+                      (sems[0].at[j, n - 1 + r], sems[1].at[j, n - 1 + r]), None, mate)
+
+    def stores(j):
+        pairs = [(l1.at[j], outs[0].at[:, :, chunk(j)])]
+        pairs += [(recv[k].at[j], outs[1 + k].at[:, :, chunk(j)]) for k in range(len(FAR))]
+        pairs.append((er.at[j], outs[5].at[:, :, :, chunk(j)]))
+        return [pltpu.make_async_copy(src, dst, out_sem.at[j, n])
+                for n, (src, dst) in enumerate(pairs)]
+
+    def send(j, _):
+        for part, ref in enumerate((k_ref, v_ref)):
+            level = halve(ref[:, chunk(j)]).astype(BF16)
+            l1[j, part] = level
+            for scr, n in zip(coarse[:3], FAR):
+                level = halve(level).astype(BF16)
+                m = BLK // n
+                scr[j, part * m:(part + 1) * m] = level
+        coarse[3][j] = jnp.concatenate(
+            [halve(coarse[2][j, :16]), halve(coarse[2][j, 16:])], 0).astype(BF16)
+        for peer in order:
+            far(j, peer).start()
+        for side in range(2):
+            @pl.when(has[side])
+            def _():
+                for part in range(2):
+                    edge(j, side, part, 1 - side).start()
+        return 0
+
+    def receive(j):
+        for peer in order:
+            if peer[1] == 1:
+                far(j, peer).wait_recv()
+            else:
+                swap(j, peer, me, core, far_sems).wait_recv()
+                swap(j, peer, me, core, swap_sems).start()
+
+    @pl.when(i == 0)
+    def _():
+        greet(peers, has, ids)
+        lax.fori_loop(0, steps, send, 0)
+        receive(0)
+
+    for peer in order:
+        if peer[1] > 1:
+            swap(i, peer, mate, 1 - core, swap_sems).wait_recv()
+    for side in range(2):
+        @pl.when(has[side])
+        def _():
+            for part in range(2):
+                edge(i, side, part, side).wait_recv()
+    for copy in stores(i):
+        copy.start()
+    here = chunk(i)
+    forward_kernel(count, q_ref, k_ref.at[:, here], v_ref.at[:, here], u_ref, gain_ref,
+                   bias_ref, l1.at[i], *[ref.at[i] for ref in recv], er.at[i], *stats)
+
+    @pl.when(i < steps - 1)
+    def _():
+        receive(i + 1)
+
+    @pl.when(i == steps - 1)
+    def _():
+        def finish(j, _):
+            for peer in order:
+                far(j, peer).wait_send()
+                if peer[1] > 1:
+                    swap(j, peer, me, core, swap_sems).wait_send()
+            for side in range(2):
+                @pl.when(has[side])
+                def _():
+                    for part in range(2):
+                        edge(j, side, part, 1 - side).wait_send()
+            for copy in stores(j):
+                copy.wait()
+            return 0
+        lax.fori_loop(0, steps, finish, 0)
 
 
 def backward_kernel(count, q_ref, k_ref, v_ref, u_ref, gain_ref, bias_ref, l1_ref,
@@ -396,16 +408,6 @@
     edge_out = shape((2, 2, BLK, cols), BF16)
     limit = 48 * 1024 * 1024
 
-    l1, *recv = pl.pallas_call(
-        functools.partial(gather_kernel, count),
-        out_shape=[shape((2, rows // 2, cols), BF16)] + piece_out + [edge_out],
-        in_specs=[vmem] * 2,
-        out_specs=[vmem] + [any_spec] * 5,
-        scratch_shapes=[pltpu.VMEM(s[1:], BF16) for s in pieces] + sem_shapes(),
-        compiler_params=pltpu.CompilerParams(
-            collective_id=0, has_side_effects=True, vmem_limit_bytes=limit),
-        name="gather_tiles",
-    )(keys_in, values_in)
     bias = score_bias(me, count)
     gain2 = gain.reshape(1, cols)
 
@@ -419,17 +421,26 @@
     lse_spec = pl.BlockSpec((HEADS_STEP, 1, rows), lambda i: (i, 0, 0))
     shared = [flat(rows)] * 4 + [flat(1), fixed(bias.shape), cube(2, rows // 2)] + piece_specs + [quad]
     params = pltpu.CompilerParams(vmem_limit_bytes=limit)
-    common = (queries, keys_in, values_in, upstream, gain2, bias, l1, *recv)
-    att, lse, stat = pl.pallas_call(
-        functools.partial(forward_kernel, count),
+    steps = grid[0]
+    dma = pltpu.SemaphoreType.DMA
+    chunks = [pltpu.VMEM((steps,) + s[:2] + (step,), BF16) for s in pieces]
+    edges = pltpu.VMEM((steps, 2, 2, BLK, step), BF16)
+    att, lse, stat, l1, *recv = pl.pallas_call(
+        functools.partial(gather_attend_kernel, count, steps),
         grid=grid,
         out_shape=[shape((rows, cols), BF16), shape((heads, 1, rows), F32),
-                   shape((2, rows, HEAD_WIDTH), F32)],
-        in_specs=shared,
-        out_specs=[flat(rows), lse_spec, fixed((2, rows, HEAD_WIDTH))],
-        compiler_params=params,
-        name="attend",
-    )(*common)
+                   shape((2, rows, HEAD_WIDTH), F32), shape((2, rows // 2, cols), BF16)]
+        + piece_out + [edge_out],
+        in_specs=[flat(rows), vmem, vmem, flat(rows), flat(1), fixed(bias.shape)],
+        out_specs=[flat(rows), lse_spec, fixed((2, rows, HEAD_WIDTH))] + [any_spec] * 6,
+        scratch_shapes=[pltpu.VMEM((steps, 2, rows // 2, step), BF16)] + chunks + [edges]
+        + [pltpu.VMEM((steps, s[1], step), BF16) for s in pieces]
+        + [dma((steps, sum(FAR)))] * 4 + [dma((steps, 2, 2))] * 2 + [dma((steps, 6))],
+        compiler_params=pltpu.CompilerParams(
+            collective_id=0, has_side_effects=True, vmem_limit_bytes=limit),
+        name="gather_and_attend",
+    )(queries, keys_in, values_in, upstream, gain2, bias)
+    common = (queries, keys_in, values_in, upstream, gain2, bias, l1, *recv)
 
     sums = jnp.sum(stat, -1)
     parts = lax.axis_size("head")
@@ -441,11 +452,8 @@
     inv = lax.rsqrt(total[0] / columns + EPSILON)
     coef = jnp.stack([inv, inv * inv * inv * total[1] / columns], 1)
 
-    steps = grid[0]
     summed = [(max(1, s[0] // 2),) + s[1:] for s in pieces]
-    chunks = [pltpu.VMEM((steps,) + s[:2] + (step,), BF16) for s in pieces]
     halves = [pltpu.VMEM((steps,) + s[:2] + (step // 2,), BF16) for s in pieces[1:]]
-    dma = pltpu.SemaphoreType.DMA
     normed, gq, loc, gl1, *back = pl.pallas_call(
         functools.partial(derive_send_kernel, count, steps),
         grid=grid,
@@ -454,7 +462,7 @@
         + [shape(s, BF16) for s in summed] + [edge_out],
         in_specs=shared + [flat(rows), lse_spec, fixed((rows, 2))],
         out_specs=[flat(rows)] * 2 + [cube(2, rows), cube(2, rows // 2)] + [any_spec] * 5,
-        scratch_shapes=chunks + [pltpu.VMEM((steps, 2, 2, BLK, step), BF16)] + halves * 2
+        scratch_shapes=chunks + [edges] + halves * 2
         + [dma((steps, sum(FAR)))] * 2 + [dma((steps, LEV - 1))] * 2 + [dma((steps, 2))] * 2,
         compiler_params=pltpu.CompilerParams(
             collective_id=1, has_side_effects=True, vmem_limit_bytes=limit),

time: 117 us -> 109 us (0.932)
  Pallas kernels: 101 us -> 95.9 us
  local copies, waits for them, and re-layouts: 11.8 us -> 8.57 us
    pallas_call x2 -> x1, Pallas kernels: 52.8 us -> 46 us  [body(): pl.pallas_call(functools.partial(gather_attend_kernel, count, steps), gri...]
    unnamed x26 -> x14, local copies, waits for them, and re-layouts: 10.8 us -> 7.58 us
    pallas_call x1, Pallas kernels: 41.7 us -> 43.8 us  [body(): pl.pallas_call(functools.partial(derive_send_kernel, count, steps), grid=...]
where the time goes in v4:
time: 109 us; the launch traced here: 108 us
  Pallas kernels  95.9 us (88%)
  local copies, waits for them, and re-layouts  8.57 us (8%)
  waiting for transfers between devices  2.21 us (2%)
    pallas_call x1, Pallas kernels, body(): pl.pallas_call(functools.partial(gather_attend_kernel, count, steps), gri...  46 us
    pallas_call x1, Pallas kernels, body(): pl.pallas_call(functools.partial(derive_send_kernel, count, steps), grid=...  43.8 us
    unnamed x14, local copies, waits for them, and re-layouts  7.58 us
    pallas_call x1, Pallas kernels, body(): pl.pallas_call(functools.partial(combine_kernel, count), grid=grid, out_s...  6.12 us
    ppermute x1, waiting for transfers between devices, body(): lax.ppermute(sums, 'head', [(i, (i + shift) % parts) for i in range(parts)])  2.21 us
  transfers between devices with their start and end apart: 1, of which 1 were waited for; matrix products, arithmetic and copies ran while one was open for 0% of the time, Pallas kernels for 0%

profile of v4, /device:TPU:13, one launch (start us, length us, event | category | flops | bytes accessed | tf_op | source)
XLA Modules:
  0.0 108.5 jit_solution(16379622303843293038)
XLA Ops:
  0.7 0.1 broadcast_in_dim.23
  0.8 0.1 reshape.247
  0.8 0.7 reshape.246.refs_4_
  1.5 0.1 fusion.1
  1.6 0.1 compare_and_fusion
  1.7 0.2 and_select_fusion
  1.9 0.1 pad_maximum_fusion.refs_5_
  2.1 46.0 %gather_and_attend.1 = (bf16[256,2560]{1,0:T(8,128)(2,1)S(1)}, f32[20,1,256]{2,1,0:T(1,128)S(1)}, f32[2,256,128]{2,1,0:T(8,128)S(1)}, bf16[2,128,2560]{2,1,0:T(8...) custom-call(bf16[256,2560]{1,0:T(8,128)(2,1)} %refs_0_.3, ...), custom_call_target="tpu_custom_call" | custom-call | tf_op jit(solution)/shard_map/gather_and_attend/pallas_call | solution.py:428
  48.1 0.0 copy-start.2
  48.1 1.0 copy-done.2
  49.1 0.0 copy-start.3
  49.1 1.1 copy-done.3
  50.2 0.1 reduce_sum.9
  50.3 0.3 collective-permute-start
  50.6 2.2 %collective-permute-done = f32[2,256]{1,0:T(2,128)S(1)} collective-permute-done((f32[2,256]{1,0:T(2,128)S(1)}, f32[2,256]{1,0:T(2,128)S(1)}, u32[]{:S(2)}, u32[]{:S(2)}) %collective-permute-start) | collective-permute-done | bytes 2080 | tf_op jit(solution)/shard_map/ppermute | solution.py:449
  52.9 0.1 copy.14.refs_14_
  53.0 43.8 %differentiate_and_send.1 = (bf16[256,2560]{1,0:T(8,128)(2,1)}, bf16[256,2560]{1,0:T(8,128)(2,1)}, f32[2,256,2560]{2,1,0:T(8,128)}, bf16[2,128,2560]{2,1,0:T(8,1...) custom-call(bf16[256,2560]{1,0:T(8,128)(2,1)} %refs_0_.3, ...), custom_call_target="tpu_custom_call" | custom-call | tf_op jit(solution)/shard_map/differentiate_and_send/pallas_call | solution.py:457
  96.9 0.0 copy-start
  96.9 1.3 %copy-done = bf16[2,128,2560]{2,1,0:T(8,128)(2,1)S(1)} copy-done((bf16[2,128,2560]{2,1,0:T(8,128)(2,1)S(1)}, bf16[2,128,2560]{2,1,0:T(8,128)(2,1)}, u32[]{:S(2)}) %copy-start) | copy-done | bytes 1310744
  98.2 0.0 copy-start.1
  98.2 1.3 %copy-done.1 = bf16[2,2,64,2560]{3,2,1,0:T(8,128)(2,1)S(1)} copy-done((bf16[2,2,64,2560]{3,2,1,0:T(8,128)(2,1)S(1)}, bf16[2,2,64,2560]{3,2,1,0:T(8,128)(2,1)}, u32[]{:S(2)}) %copy-start.1) | copy-done | bytes 1310744
  99.5 0.0 copy-start.5
  99.5 6.1 %combine.1 = (bf16[256,2560]{1,0:T(8,128)(2,1)}, bf16[256,2560]{1,0:T(8,128)(2,1)}) custom-call(f32[2,256,2560]{2,1,0:T(8,128)} %get-tuple-element.35.loc_ref, bf16[2,128,2560]{2,1,0:T(8,128)(2,1)S(1)} %copy-done, bf16[1,128,2560]{2,1,0:T(8,128)(2,1)S(1)} %get-tuple-element.37.r2, bf16[1,64,2560]{2,1,0:T(8,128)(2,1)S(1)} %get-tuple-element.38.r3, ...), custom_call_target="tpu_custom_call" | custom-call | tf_op jit(solution)/shard_map/combine/pallas_call | solution.py:472
  105.6 0.0 copy-done.5
  105.6 0.0 copy-start.4
  105.6 1.1 copy.17
  106.7 0.7 copy-done.4
  107.4 1.1 copy.18
  (8 shorter events, 0.1 us)
Async XLA Ops:
  48.1 1.1 copy-start.2
  49.1 1.1 copy-start.3
  50.3 2.5 %collective-permute-start = (f32[2,256]{1,0:T(2,128)S(1)}, f32[2,256]{1,0:T(2,128)S(1)}, u32[]{:S(2)}, u32[]{:S(2)}) collective-permute-start(f32[2,256]{1,0:T(2,128)S(1)} %reduce_sum.9), channel_id=1, source_target_pairs={{0,1},{1,0},{2,3},{3,2},{4,5},{5,4},{6,7},{7,6},{8,9},{9,8},{10,11... | collective-permute-start | bytes 6152 | tf_op jit(solution)/shard_map/ppermute | solution.py:449
  96.9 1.3 %copy-start = (bf16[2,128,2560]{2,1,0:T(8,128)(2,1)S(1)}, bf16[2,128,2560]{2,1,0:T(8,128)(2,1)}, u32[]{:S(2)}) copy-start(bf16[2,128,2560]{2,1,0:T(8,128)(2,1)} %get-tuple-element.36.gl1_ref) | copy-start | bytes 3932164
  98.2 1.3 %copy-start.1 = (bf16[2,2,64,2560]{3,2,1,0:T(8,128)(2,1)S(1)}, bf16[2,2,64,2560]{3,2,1,0:T(8,128)(2,1)}, u32[]{:S(2)}) copy-start(bf16[2,2,64,2560]{3,2,1,0:T(8,128)(2,1)} %get-tuple-element.41.er_ref) | copy-start | bytes 3932164
  99.5 6.1 %copy-start.5 = (bf16[256,2560]{1,0:T(8,128)(2,1)S(1)}, bf16[256,2560]{1,0:T(8,128)(2,1)}, u32[]{:S(2)}) copy-start(bf16[256,2560]{1,0:T(8,128)(2,1)} %get-tuple-element.54) | copy-start | bytes 3932164
  105.6 1.8 %copy-start.4 = (bf16[256,2560]{1,0:T(8,128)(2,1)S(1)}, bf16[256,2560]{1,0:T(8,128)(2,1)}, u32[]{:S(2)}) copy-start(bf16[256,2560]{1,0:T(8,128)(2,1)} %get-tuple-element.55) | copy-start | bytes 3932164

commit v5 on v4

--- a/solution.py
+++ b/solution.py
@@ -267,7 +267,7 @@
             eg_ref[0, part, :, c] = a[:BLK].astype(BF16)
             eg_ref[1, part, :, c] = b[3 * BLK:4 * BLK].astype(BF16)
             loc_ref[part, :, c] = jnp.concatenate(
-                [a[BLK:2 * BLK], a[2 * BLK:4 * BLK] + b[:2 * BLK], b[2 * BLK:3 * BLK]], 0)
+                [a[BLK:2 * BLK], a[2 * BLK:4 * BLK] + b[:2 * BLK], b[2 * BLK:3 * BLK]], 0).astype(BF16)
             gl1_ref[part, :, c] = jnp.concatenate(
                 [b[4 * BLK:5 * BLK], a[4 * BLK:5 * BLK]], 0).astype(BF16)
         both = [terms[0][part][5 * BLK:] + terms[1][part][5 * BLK:] for part in range(2)]
@@ -376,7 +376,7 @@
             else:
                 wide = ref[...].astype(F32)
                 far.append(wide[:, part * m:(part + 1) * m].reshape(-1, span).astype(BF16))
-        total = loc_ref[part] + dot(mat, jnp.concatenate(far, 0), NN)
+        total = loc_ref[part].astype(F32) + dot(mat, jnp.concatenate(far, 0), NN)
         low = jnp.where(flags[0], er_ref[0, part].astype(F32), 0.0)
         high = jnp.where(flags[1], er_ref[1, part].astype(F32), 0.0)
         out[:BLK] = (total[:BLK] + low).astype(BF16)
@@ -458,7 +458,7 @@
         functools.partial(derive_send_kernel, count, steps),
         grid=grid,
         out_shape=[shape((rows, cols), BF16)] * 2
-        + [shape((2, rows, cols), F32), shape((2, rows // 2, cols), BF16)]
+        + [shape((2, rows, cols), BF16), shape((2, rows // 2, cols), BF16)]
         + [shape(s, BF16) for s in summed] + [edge_out],
         in_specs=shared + [flat(rows), lse_spec, fixed((rows, 2))],
         out_specs=[flat(rows)] * 2 + [cube(2, rows), cube(2, rows // 2)] + [any_spec] * 5,

time: 109 us -> 108 us (level)
  no operation moved by 1% of the time
where the time goes in v5:
time: 108 us
  Pallas kernels  95.1 us (88%)
  local copies, waits for them, and re-layouts  8.57 us (8%)
  waiting for transfers between devices  2.21 us (2%)
    pallas_call x1, Pallas kernels, body(): pl.pallas_call(functools.partial(gather_attend_kernel, count, steps), gri...  46 us
    pallas_call x1, Pallas kernels, body(): pl.pallas_call(functools.partial(derive_send_kernel, count, steps), grid=...  43.6 us
    unnamed x14, local copies, waits for them, and re-layouts  7.58 us
    pallas_call x1, Pallas kernels, body(): pl.pallas_call(functools.partial(combine_kernel, count), grid=grid, out_s...  5.56 us
    ppermute x1, waiting for transfers between devices, body(): lax.ppermute(sums, 'head', [(i, (i + shift) % parts) for i in range(parts)])  2.21 us
  transfers between devices with their start and end apart: 1, of which 1 were waited for; matrix products, arithmetic and copies ran while one was open for 0% of the time, Pallas kernels for 0%

profile of v5, /device:TPU:13, one launch (start us, length us, event | category | flops | bytes accessed | tf_op | source)
XLA Modules:
  0.0 107.7 jit_solution(17453412209110868692)
XLA Ops:
  0.7 0.1 broadcast_in_dim.23
  0.8 0.1 reshape.247
  0.8 0.7 reshape.246.refs_4_
  1.5 0.1 fusion.1
  1.6 0.1 compare_and_fusion
  1.7 0.2 and_select_fusion
  1.9 0.1 pad_maximum_fusion.refs_5_
  2.1 46.0 %gather_and_attend.1 = (bf16[256,2560]{1,0:T(8,128)(2,1)S(1)}, f32[20,1,256]{2,1,0:T(1,128)S(1)}, f32[2,256,128]{2,1,0:T(8,128)S(1)}, bf16[2,128,2560]{2,1,0:T(8...) custom-call(bf16[256,2560]{1,0:T(8,128)(2,1)} %refs_0_.3, ...), custom_call_target="tpu_custom_call" | custom-call | tf_op jit(solution)/shard_map/gather_and_attend/pallas_call | solution.py:428
  48.1 0.0 copy-start.2
  48.1 1.0 copy-done.2
  49.1 0.0 copy-start.3
  49.1 1.1 copy-done.3
  50.2 0.1 reduce_sum.9
  50.3 0.3 collective-permute-start
  50.6 2.2 %collective-permute-done = f32[2,256]{1,0:T(2,128)S(1)} collective-permute-done((f32[2,256]{1,0:T(2,128)S(1)}, f32[2,256]{1,0:T(2,128)S(1)}, u32[]{:S(2)}, u32[]{:S(2)}) %collective-permute-start) | collective-permute-done | bytes 2080 | tf_op jit(solution)/shard_map/ppermute | solution.py:449
  52.9 0.1 copy.14.refs_14_
  53.0 43.6 %differentiate_and_send.1 = (bf16[256,2560]{1,0:T(8,128)(2,1)}, bf16[256,2560]{1,0:T(8,128)(2,1)}, bf16[2,256,2560]{2,1,0:T(8,128)(2,1)}, bf16[2,128,2560]{2,1,0...) custom-call(bf16[256,2560]{1,0:T(8,128)(2,1)} %refs_0_.3, ...), custom_call_target="tpu_custom_call" | custom-call | tf_op jit(solution)/shard_map/differentiate_and_send/pallas_call | solution.py:457
  96.6 0.0 copy-start
  96.6 1.3 %copy-done = bf16[2,128,2560]{2,1,0:T(8,128)(2,1)S(1)} copy-done((bf16[2,128,2560]{2,1,0:T(8,128)(2,1)S(1)}, bf16[2,128,2560]{2,1,0:T(8,128)(2,1)}, u32[]{:S(2)}) %copy-start) | copy-done | bytes 1310744
  97.9 0.0 copy-start.1
  97.9 1.3 %copy-done.1 = bf16[2,2,64,2560]{3,2,1,0:T(8,128)(2,1)S(1)} copy-done((bf16[2,2,64,2560]{3,2,1,0:T(8,128)(2,1)S(1)}, bf16[2,2,64,2560]{3,2,1,0:T(8,128)(2,1)}, u32[]{:S(2)}) %copy-start.1) | copy-done | bytes 1310744
  99.2 0.0 copy-start.5
  99.2 5.6 %combine.1 = (bf16[256,2560]{1,0:T(8,128)(2,1)}, bf16[256,2560]{1,0:T(8,128)(2,1)}) custom-call(bf16[2,256,2560]{2,1,0:T(8,128)(2,1)} %get-tuple-element.35.loc_ref, bf16[2,128,2560]{2,1,0:T(8,128)(2,1)S(1)} %copy-done, bf16[1,128,2560]{2,1,0:T(8,128)(2,1)S(1)} %get-tuple-element.37.r2, bf16[1,64,2560]{2,1,0:T(8,128)(2,1)S(1)} %get-tuple-element.38.r3, ...), custom_call_target="tpu_custom_call" | custom-call | tf_op jit(solution)/shard_map/combine/pallas_call | solution.py:472
  104.8 0.0 copy-done.5
  104.8 0.0 copy-start.4
  104.8 1.1 copy.17
  105.9 0.7 copy-done.4
  106.6 1.1 copy.18
  (8 shorter events, 0.1 us)
Async XLA Ops:
  48.1 1.1 copy-start.2
  49.1 1.1 copy-start.3
  50.3 2.5 %collective-permute-start = (f32[2,256]{1,0:T(2,128)S(1)}, f32[2,256]{1,0:T(2,128)S(1)}, u32[]{:S(2)}, u32[]{:S(2)}) collective-permute-start(f32[2,256]{1,0:T(2,128)S(1)} %reduce_sum.9), channel_id=1, source_target_pairs={{0,1},{1,0},{2,3},{3,2},{4,5},{5,4},{6,7},{7,6},{8,9},{9,8},{10,11... | collective-permute-start | bytes 6152 | tf_op jit(solution)/shard_map/ppermute | solution.py:449
  96.6 1.3 %copy-start = (bf16[2,128,2560]{2,1,0:T(8,128)(2,1)S(1)}, bf16[2,128,2560]{2,1,0:T(8,128)(2,1)}, u32[]{:S(2)}) copy-start(bf16[2,128,2560]{2,1,0:T(8,128)(2,1)} %get-tuple-element.36.gl1_ref) | copy-start | bytes 3932164
  97.9 1.3 %copy-start.1 = (bf16[2,2,64,2560]{3,2,1,0:T(8,128)(2,1)S(1)}, bf16[2,2,64,2560]{3,2,1,0:T(8,128)(2,1)}, u32[]{:S(2)}) copy-start(bf16[2,2,64,2560]{3,2,1,0:T(8,128)(2,1)} %get-tuple-element.41.er_ref) | copy-start | bytes 3932164
  99.2 5.6 %copy-start.5 = (bf16[256,2560]{1,0:T(8,128)(2,1)S(1)}, bf16[256,2560]{1,0:T(8,128)(2,1)}, u32[]{:S(2)}) copy-start(bf16[256,2560]{1,0:T(8,128)(2,1)} %get-tuple-element.54) | copy-start | bytes 3932164
  104.8 1.8 %copy-start.4 = (bf16[256,2560]{1,0:T(8,128)(2,1)S(1)}, bf16[256,2560]{1,0:T(8,128)(2,1)}, u32[]{:S(2)}) copy-start(bf16[256,2560]{1,0:T(8,128)(2,1)} %get-tuple-element.55) | copy-start | bytes 3932164
